TPU v7x, 32 devices: a whole 2x2x4 slice. The times are simulated.
32 devices in a mesh: dp: 8 (over z, y), section: 4 (over x, core).
Axes of the slice: x: 2, y: 2, z: 4, core: 2. Of those that a mesh axis runs over, the one named last changes fastest.
Arguments:
- encoder_in: bfloat16 [16, 512, 768], P('dp'), may hold values from -6 to 6
- decoder_in: bfloat16 [16, 96, 768], P('dp'), may hold values from -6 to 6
- lengths: int32 [16, 3], P('dp'), may hold values from 64 to 384, as said below
- query_map: int32 [16, 3], P('dp'), may hold values from 0 to 2, as said below
- attn_query: bfloat16 [3, 768, 768], P(None, 'section'), may hold values from -0.02734375 to 0.02734375
- attn_keyval: bfloat16 [6, 768, 768], P(None, 'section'), may hold values from -0.21875 to 0.21875
- attn_output: bfloat16 [3, 768, 768], P(None, 'section'), may hold values from -0.875 to 0.875
- feed_in: bfloat16 [2, 3072, 768], P(None, 'section'), may hold values from -0.21875 to 0.21875
- feed_out: bfloat16 [2, 3072, 768], P(None, 'section'), may hold values from -0.109375 to 0.109375
- norm_gains: float32 [5, 768], replicated, may hold values from 0.5 to 1.5
- position_bias: float32 [2, 32, 12], replicated, may hold values from -4 to 4
- cotangent: bfloat16 [16, 96, 768], P('dp'), may hold values from -6 to 6
Outputs:
- decoder_out: bfloat16 [16, 96, 768], P('dp', 'section')
- encoder_in_grad: bfloat16 [16, 512, 768], P('dp', 'section')
- decoder_in_grad: bfloat16 [16, 96, 768], P('dp', 'section')
- attn_query_grad: float32 [3, 768, 768], P(None, 'section')
- attn_keyval_grad: float32 [6, 768, 768], P(None, 'section')
- attn_output_grad: float32 [3, 768, 768], P(None, 'section')
- feed_in_grad: float32 [2, 3072, 768], P(None, 'section')
- feed_out_grad: float32 [2, 3072, 768], P(None, 'section')
- norm_gains_grad: float32 [5, 768], replicated
- position_bias_grad: float32 [2, 32, 12], replicated
Inputs may be any that keep to these rules, and one draw needn't show every extreme that they name: In every buffer the 3 lengths sum to 512, and the longest is exactly 384. `query_map`: in every buffer each of the 3 queries owns at least one passage.
All inputs are finite; a program needn't handle non-finite values.
Results may differ from a plain program's by a relative error of at most 0.028.
Values may be sent and summed in bfloat16 or wider, within the bound.
No kernel may reach another device: no remote copies, remote signals or barrier semaphores. Data moves between devices by JAX's collectives and lax.ppermute only.
A program may use at most 640 MiB of HBM per device.

v0:
```python
import jax
import jax.numpy as jnp
from jax import lax
from jax.sharding import PartitionSpec as P

D = 768
HEADS = 12
HD = 64
NB = 32
BUF = 512
PASS = 3
QPB = 3
TGT = 32
MICRO = 2
MBUF = 1


epsilon = 1e-06
masked_score = -1e30
query_block = 512
enc_edges = (12, 16, 23, 32, 46, 64, 91)
dec_edges = (19, 21, 24, 27, 31)


def for_sending(array):
    return jax.tree.map(lambda a: a.astype(jnp.bfloat16) if a.dtype == jnp.float32 else a, array)


def from_behind(value, axis, steps):
    count = lax.axis_size(axis)
    first, last = (max(0, -steps), min(count, count - steps))
    return lax.ppermute(value, axis, [(source, source + steps) for source in range(first, last)])


def norm_piece(rows, gain):
    return rows * lax.rsqrt(jnp.mean(rows * rows, axis=-1, keepdims=True) + epsilon) * gain


def gelu_piece(hidden):
    return jax.nn.gelu(hidden, approximate=True)


def matmul(left, right):
    return jnp.dot(left, right, preferred_element_type=jnp.float32)


def matmul_right_t(left, right):
    return lax.dot_general(
        left, right, (((1,), (1,)), ((), ())), preferred_element_type=jnp.float32
    )


def matmul_left_t(left, right):
    return lax.dot_general(
        left, right, (((0,), (0,)), ((), ())), preferred_element_type=jnp.float32
    )


def encoder_bucket(offset):
    distance = jnp.abs(offset)
    bucket = jnp.minimum(distance, 8)
    for boundary in enc_edges:
        bucket = bucket + (distance >= boundary).astype(jnp.int32)
    return bucket + 16 * (offset > 0).astype(jnp.int32)


def decoder_bucket(offset):
    distance = jnp.maximum(-offset, 0)
    bucket = jnp.minimum(distance, 16)
    for boundary in dec_edges:
        bucket = bucket + (distance >= boundary).astype(jnp.int32)
    return bucket


def full_bias(table, bucket_fn, count):
    positions = jnp.arange(count, dtype=jnp.int32)
    bucket = bucket_fn(positions[None, :] - positions[:, None])
    return jnp.take(jnp.transpose(table), bucket, axis=1)


def split_heads(rows):
    return rows.reshape(rows.shape[0], HEADS, HD)


def block_scores(query_rows, keys_rows, allowed, bias_block):
    scores = jnp.einsum(
        "rhd,chd->hrc",
        split_heads(query_rows),
        split_heads(keys_rows),
        preferred_element_type=jnp.float32,
    )
    if bias_block is not None:
        scores = scores + bias_block
    return jnp.where(allowed[None], scores, masked_score)


def attend_forward(queries, keys_rows, values_rows, layout, bias_all):
    total = queries.shape[0]
    width = min(query_block, total)
    contexts = []
    log_sums = []
    for first_row in range(0, total, width):
        allowed, bucket = layout(first_row, width)
        bias_block = None if bias_all is None else bias_all
        scores = block_scores(
            queries[first_row : first_row + width], keys_rows, allowed, bias_block
        )
        row_peak = jnp.max(scores, axis=-1, keepdims=True)
        raised = jnp.exp(scores - row_peak)
        row_total = jnp.sum(raised, axis=-1, keepdims=True)
        weights = (raised / row_total).astype(jnp.bfloat16)
        context = jnp.einsum(
            "hrc,chd->rhd", weights, split_heads(values_rows), preferred_element_type=jnp.float32
        )
        contexts.append(context.reshape(width, D))
        log_sums.append(row_peak[:, :, 0] + jnp.log(row_total[:, :, 0]))
    return (
        jnp.concatenate(contexts, axis=0).astype(jnp.bfloat16),
        jnp.concatenate(log_sums, axis=1),
    )


def attend_backward(queries, keys_rows, values_rows, log_sums, grad_context, layout, bias_all):
    total = queries.shape[0]
    width = min(query_block, total)
    columns = keys_rows.shape[0]
    grad_queries = []
    grad_keys = jnp.zeros((columns, HEADS, HD), jnp.float32)
    grad_values = jnp.zeros((columns, HEADS, HD), jnp.float32)
    grad_table = jnp.zeros((NB, HEADS), jnp.float32)
    for first_row in range(0, total, width):
        allowed, bucket = layout(first_row, width)
        query_rows = queries[first_row : first_row + width]
        bias_block = None if bias_all is None else bias_all
        scores = block_scores(query_rows, keys_rows, allowed, bias_block)
        probs = jnp.exp(scores - log_sums[:, first_row : first_row + width, None])
        grad_rows = split_heads(grad_context[first_row : first_row + width])
        grad_probs = jnp.einsum(
            "rhd,chd->hrc", grad_rows, split_heads(values_rows), preferred_element_type=jnp.float32
        )
        grad_scores = probs * (grad_probs - jnp.sum(probs * grad_probs, axis=-1, keepdims=True))
        grad_scores = grad_scores.astype(jnp.bfloat16)
        grad_queries.append(
            jnp.einsum(
                "hrc,chd->rhd",
                grad_scores,
                split_heads(keys_rows),
                preferred_element_type=jnp.float32,
            ).reshape(width, D)
        )
        grad_keys = grad_keys + jnp.einsum(
            "hrc,rhd->chd", grad_scores, split_heads(query_rows), preferred_element_type=jnp.float32
        )
        grad_values = grad_values + jnp.einsum(
            "hrc,rhd->chd",
            probs.astype(jnp.bfloat16),
            grad_rows,
            preferred_element_type=jnp.float32,
        )
        if bias_all is not None:
            onehot = (bucket[:, :, None] == jnp.arange(NB, dtype=jnp.int32)[None, None, :]).astype(
                jnp.bfloat16
            )
            grad_table = grad_table + jnp.einsum(
                "hrc,rcb->bh", grad_scores, onehot, preferred_element_type=jnp.float32
            )
    return (
        jnp.concatenate(grad_queries, axis=0).astype(jnp.bfloat16),
        grad_keys.reshape(columns, D).astype(jnp.bfloat16),
        grad_values.reshape(columns, D).astype(jnp.bfloat16),
        grad_table,
    )


def attend_buffers(queries, keys_rows, values_rows, extra, make_layout, bias_all):
    count = extra.shape[0]

    def one_buffer(items):
        query_buf, key_buf, value_buf, extra_buf = items
        return attend_forward(query_buf, key_buf, value_buf, make_layout(extra_buf), bias_all)

    context, log_sums = lax.map(
        one_buffer,
        (
            queries.reshape(count, -1, D),
            keys_rows.reshape(count, -1, D),
            values_rows.reshape(count, -1, D),
            extra,
        ),
    )
    return (context.reshape(-1, D), log_sums)


def attend_buffers_back(
    queries, keys_rows, values_rows, extra, log_sums, grad_context, make_layout, bias_all
):
    count = extra.shape[0]

    def one_buffer(items):
        query_buf, key_buf, value_buf, extra_buf, sums_buf, grad_buf = items
        return attend_backward(
            query_buf, key_buf, value_buf, sums_buf, grad_buf, make_layout(extra_buf), bias_all
        )

    grad_queries, grad_keys, grad_values, grad_table = lax.map(
        one_buffer,
        (
            queries.reshape(count, -1, D),
            keys_rows.reshape(count, -1, D),
            values_rows.reshape(count, -1, D),
            extra,
            log_sums,
            grad_context.reshape(count, -1, D),
        ),
    )
    return (
        grad_queries.reshape(-1, D),
        grad_keys.reshape(-1, D),
        grad_values.reshape(-1, D),
        jnp.sum(grad_table, axis=0),
    )


def encoder_layout(segment):

    def layout(first_row, count):
        rows_pos = first_row + jnp.arange(count, dtype=jnp.int32)
        cols_pos = jnp.arange(segment.shape[0], dtype=jnp.int32)
        allowed = segment[first_row : first_row + count, None] == segment[None, :]
        return (allowed, encoder_bucket(cols_pos[None, :] - rows_pos[:, None]))

    return layout


def decoder_layout(ignored):

    def layout(first_row, count):
        rows_pos = first_row + jnp.arange(count, dtype=jnp.int32)
        cols_pos = jnp.arange(QPB * TGT, dtype=jnp.int32)
        offset = cols_pos[None, :] - rows_pos[:, None]
        allowed = (rows_pos[:, None] // TGT == cols_pos[None, :] // TGT) & (offset <= 0)
        return (allowed, decoder_bucket(offset))

    return layout


def cross_layout(owner):

    def layout(first_row, count):
        rows_pos = first_row + jnp.arange(count, dtype=jnp.int32)
        return (rows_pos[:, None] // TGT == owner[None, :], None)

    return layout


def encoder_attention(owned, norm_gains, position_bias, inputs, segment, grad_sent):
    bias_all = full_bias(position_bias[0], encoder_bucket, BUF)
    rows = inputs.reshape(-1, D).astype(jnp.float32)
    normed, norm_back = jax.vjp(norm_piece, rows, norm_gains[0])
    normed = normed.astype(jnp.bfloat16)
    queries = matmul(normed, owned[0]).astype(jnp.bfloat16)
    keys_rows = matmul(normed, owned[1]).astype(jnp.bfloat16)
    values_rows = matmul(normed, owned[2]).astype(jnp.bfloat16)
    context, log_sums = attend_buffers(
        queries, keys_rows, values_rows, segment, encoder_layout, bias_all
    )
    sent = (rows + matmul(context, owned[3])).astype(jnp.bfloat16).reshape(inputs.shape)
    if grad_sent is None:
        return sent
    grad_rows = grad_sent.reshape(-1, D)
    grad_output_w = matmul_left_t(context, grad_rows)
    grad_context = matmul_right_t(grad_rows, owned[3]).astype(jnp.bfloat16)
    grad_queries, grad_keys, grad_values, grad_table = attend_buffers_back(
        queries, keys_rows, values_rows, segment, log_sums, grad_context, encoder_layout, bias_all
    )
    grad_normed = (
        matmul_right_t(grad_queries, owned[0])
        + matmul_right_t(grad_keys, owned[1])
        + matmul_right_t(grad_values, owned[2])
    )
    grad_inputs, grad_gain = norm_back(grad_normed)
    grad_inputs = grad_inputs + grad_rows.astype(jnp.float32)
    empty = jnp.zeros_like(grad_output_w)
    blocks_grad = jnp.stack(
        [
            matmul_left_t(normed, grad_queries),
            matmul_left_t(normed, grad_keys),
            matmul_left_t(normed, grad_values),
            grad_output_w,
            empty,
            empty,
            empty,
            empty,
        ]
    )
    return (
        grad_inputs.astype(jnp.bfloat16).reshape(inputs.shape),
        blocks_grad,
        grad_gain,
        grad_table,
    )


def feed_section(owned, gain, inputs, grad_sent):
    weight_in = owned[0:4].reshape(-1, D)
    weight_out = owned[4:8].reshape(-1, D)
    rows = inputs.reshape(-1, D).astype(jnp.float32)
    normed, norm_back = jax.vjp(norm_piece, rows, gain)
    normed = normed.astype(jnp.bfloat16)
    hidden = matmul_right_t(normed, weight_in)
    active, gelu_back = jax.vjp(gelu_piece, hidden)
    active = active.astype(jnp.bfloat16)
    output = (rows + matmul(active, weight_out)).astype(jnp.bfloat16).reshape(inputs.shape)
    if grad_sent is None:
        return output
    grad_rows = grad_sent.reshape(-1, D)
    grad_out_w = matmul_left_t(active, grad_rows)
    grad_hidden = gelu_back(matmul_right_t(grad_rows, weight_out))[0].astype(jnp.bfloat16)
    grad_in_w = matmul_left_t(grad_hidden, normed)
    grad_inputs, grad_gain = norm_back(matmul(grad_hidden, weight_in))
    grad_inputs = grad_inputs + grad_rows.astype(jnp.float32)
    blocks_grad = jnp.concatenate([grad_in_w.reshape(4, D, D), grad_out_w.reshape(4, D, D)])
    return (output, grad_inputs.astype(jnp.bfloat16).reshape(inputs.shape), blocks_grad, grad_gain)


def decoder_attention(owned, norm_gains, position_bias, inputs, encoded, owner, grad_sent):
    bias_all = full_bias(position_bias[1], decoder_bucket, QPB * TGT)
    rows = inputs.reshape(-1, D).astype(jnp.float32)
    first_norm, first_back = jax.vjp(norm_piece, rows, norm_gains[2])
    first_norm = first_norm.astype(jnp.bfloat16)
    queries = matmul(first_norm, owned[0]).astype(jnp.bfloat16)
    keys_rows = matmul(first_norm, owned[1]).astype(jnp.bfloat16)
    values_rows = matmul(first_norm, owned[2]).astype(jnp.bfloat16)
    self_context, self_sums = attend_buffers(
        queries, keys_rows, values_rows, owner, decoder_layout, bias_all
    )
    middle = rows + matmul(self_context, owned[3])
    second_norm, second_back = jax.vjp(norm_piece, middle, norm_gains[3])
    second_norm = second_norm.astype(jnp.bfloat16)
    cross_queries = matmul(second_norm, owned[4]).astype(jnp.bfloat16)
    encoded_rows = encoded.reshape(-1, D)
    cross_keys = matmul(encoded_rows, owned[5]).astype(jnp.bfloat16)
    cross_values = matmul(encoded_rows, owned[6]).astype(jnp.bfloat16)
    cross_context, cross_sums = attend_buffers(
        cross_queries, cross_keys, cross_values, owner, cross_layout, None
    )
    sent = (middle + matmul(cross_context, owned[7])).astype(jnp.bfloat16).reshape(inputs.shape)
    if grad_sent is None:
        return sent
    grad_rows = grad_sent.reshape(-1, D)
    grad_cross_out = matmul_left_t(cross_context, grad_rows)
    grad_cross_context = matmul_right_t(grad_rows, owned[7]).astype(jnp.bfloat16)
    grad_cross_queries, grad_cross_keys, grad_cross_values, unused = attend_buffers_back(
        cross_queries,
        cross_keys,
        cross_values,
        owner,
        cross_sums,
        grad_cross_context,
        cross_layout,
        None,
    )
    grad_encoded = (
        matmul_right_t(grad_cross_keys, owned[5]) + matmul_right_t(grad_cross_values, owned[6])
    ).astype(jnp.bfloat16)
    grad_middle, gain_cross = second_back(matmul_right_t(grad_cross_queries, owned[4]))
    grad_middle = grad_middle + grad_rows.astype(jnp.float32)
    grad_middle_low = grad_middle.astype(jnp.bfloat16)
    grad_self_out = matmul_left_t(self_context, grad_middle_low)
    grad_self_context = matmul_right_t(grad_middle_low, owned[3]).astype(jnp.bfloat16)
    grad_queries, grad_keys, grad_values, grad_table = attend_buffers_back(
        queries,
        keys_rows,
        values_rows,
        owner,
        self_sums,
        grad_self_context,
        decoder_layout,
        bias_all,
    )
    grad_normed = (
        matmul_right_t(grad_queries, owned[0])
        + matmul_right_t(grad_keys, owned[1])
        + matmul_right_t(grad_values, owned[2])
    )
    grad_inputs, gain_self = first_back(grad_normed)
    grad_inputs = grad_inputs + grad_middle
    blocks_grad = jnp.stack(
        [
            matmul_left_t(first_norm, grad_queries),
            matmul_left_t(first_norm, grad_keys),
            matmul_left_t(first_norm, grad_values),
            grad_self_out,
            matmul_left_t(second_norm, grad_cross_queries),
            matmul_left_t(encoded_rows, grad_cross_keys),
            matmul_left_t(encoded_rows, grad_cross_values),
            grad_cross_out,
        ]
    )
    return (
        grad_inputs.astype(jnp.bfloat16).reshape(inputs.shape),
        grad_encoded.reshape(encoded.shape),
        blocks_grad,
        gain_self,
        gain_cross,
        grad_table,
    )


def unpack_home(home):
    query_grad = jnp.stack([home[0, 0], home[2, 0], home[2, 4]])
    keyval_grad = jnp.stack(
        [home[0, 1], home[0, 2], home[2, 1], home[2, 2], home[2, 5], home[2, 6]]
    )
    output_grad = jnp.stack([home[0, 3], home[2, 3], home[2, 7]])
    feed_in_grad = jnp.stack([home[1, 0:4].reshape(-1, D), home[3, 0:4].reshape(-1, D)])
    feed_out_grad = jnp.stack([home[1, 4:8].reshape(-1, D), home[3, 4:8].reshape(-1, D)])
    return (query_grad, keyval_grad, output_grad, feed_in_grad, feed_out_grad)


def shards(
    encoder_in,
    decoder_in,
    lengths,
    query_map,
    attn_query,
    attn_keyval,
    attn_output,
    feed_in,
    feed_out,
    norm_gains,
    position_bias,
    cotangent,
):
    quarter = D // lax.axis_size("section")
    section_id = lax.axis_index("section")
    dec_rows = QPB * TGT
    empty_blocks = jnp.zeros((4, quarter, D), jnp.bfloat16)
    packed = jnp.stack(
        [
            jnp.concatenate([attn_query[0:1], attn_keyval[0:2], attn_output[0:1], empty_blocks]),
            jnp.concatenate(
                [feed_in[0].reshape(4, quarter, D), feed_out[0].reshape(4, quarter, D)]
            ),
            jnp.concatenate(
                [
                    attn_query[1:2],
                    attn_keyval[2:4],
                    attn_output[1:2],
                    attn_query[2:3],
                    attn_keyval[4:6],
                    attn_output[2:3],
                ]
            ),
            jnp.concatenate(
                [feed_in[1].reshape(4, quarter, D), feed_out[1].reshape(4, quarter, D)]
            ),
        ]
    )
    owned = lax.all_to_all(packed, "section", split_axis=0, concat_axis=2, tiled=True)[0]
    zero_enc = jnp.zeros((MBUF, BUF, D), jnp.bfloat16)
    zero_dec = jnp.zeros((MBUF, dec_rows, D), jnp.bfloat16)
    zero_gains = jnp.zeros((5, D), jnp.float32)
    zero_tables = jnp.zeros((2, NB, HEADS), jnp.float32)
    zero_blocks = jnp.zeros((8, D, D), jnp.float32)

    def slice_rows(array, slot_id):
        return lax.dynamic_slice_in_dim(array, slot_id * MBUF, MBUF, 0)

    def micro_layout(slot_id):
        lengths_rows = slice_rows(lengths, slot_id)
        owners_rows = slice_rows(query_map, slot_id)
        positions = jnp.arange(BUF, dtype=jnp.int32)
        ends = jnp.cumsum(lengths_rows, axis=1)
        segment = jnp.sum((positions[None, :, None] >= ends[:, None, :]).astype(jnp.int32), axis=2)
        choose = segment[:, :, None] == jnp.arange(PASS, dtype=jnp.int32)[None, None, :]
        owner = jnp.sum(jnp.where(choose, owners_rows[:, None, :], 0), axis=2)
        return (segment, owner)

    def forward_zero(carry_enc, carry_dec, slot_id):
        segment, owner = micro_layout(slot_id)
        return (
            encoder_attention(
                owned, norm_gains, position_bias, slice_rows(encoder_in, slot_id), segment, None
            ),
            zero_dec,
        )

    def forward_one(carry_enc, carry_dec, slot_id):
        return (feed_section(owned, norm_gains[1], carry_enc, None), zero_dec)

    def forward_two(carry_enc, carry_dec, slot_id):
        segment, owner = micro_layout(slot_id)
        return (
            zero_enc,
            decoder_attention(
                owned,
                norm_gains,
                position_bias,
                slice_rows(decoder_in, slot_id),
                carry_enc,
                owner,
                None,
            ),
        )

    def forward_three(carry_enc, carry_dec, slot_id):
        return (zero_enc, zero_dec)

    def backward_zero(kept_e, kept_d, grad_enc, grad_dec, slot_id):
        segment, owner = micro_layout(slot_id)
        grad_inputs, blocks_grad, gain_grad, table_grad = encoder_attention(
            owned, norm_gains, position_bias, slice_rows(encoder_in, slot_id), segment, grad_enc
        )
        return (
            zero_enc,
            zero_dec,
            grad_inputs,
            zero_dec,
            zero_dec,
            blocks_grad,
            zero_gains.at[0].set(gain_grad),
            zero_tables.at[0].set(table_grad),
        )

    def backward_one(kept_e, kept_d, grad_enc, grad_dec, slot_id):
        output, grad_inputs, blocks_grad, gain_grad = feed_section(
            owned, norm_gains[1], kept_e, grad_enc
        )
        return (
            grad_inputs,
            zero_dec,
            zero_enc,
            zero_dec,
            zero_dec,
            blocks_grad,
            zero_gains.at[1].set(gain_grad),
            zero_tables,
        )

    def backward_two(kept_e, kept_d, grad_enc, grad_dec, slot_id):
        segment, owner = micro_layout(slot_id)
        grad_inputs, grad_encoded, blocks_grad, gain_self, gain_cross, table_grad = (
            decoder_attention(
                owned,
                norm_gains,
                position_bias,
                slice_rows(decoder_in, slot_id),
                kept_e,
                owner,
                grad_dec,
            )
        )
        gains_grad = zero_gains.at[2].set(gain_self).at[3].set(gain_cross)
        return (
            grad_encoded,
            zero_dec,
            zero_enc,
            zero_dec,
            grad_inputs,
            blocks_grad,
            gains_grad,
            zero_tables.at[1].set(table_grad),
        )

    def backward_three(kept_e, kept_d, grad_enc, grad_dec, slot_id):
        output, grad_inputs, blocks_grad, gain_grad = feed_section(
            owned, norm_gains[4], kept_d, slice_rows(cotangent, slot_id)
        )
        return (
            zero_enc,
            grad_inputs,
            zero_enc,
            output,
            zero_dec,
            blocks_grad,
            zero_gains.at[4].set(gain_grad),
            zero_tables,
        )

    def backward_nothing(kept_e, kept_d, grad_enc, grad_dec, slot_id):
        return (
            zero_enc,
            zero_dec,
            zero_enc,
            zero_dec,
            zero_dec,
            zero_blocks,
            zero_gains,
            zero_tables,
        )

    carry_enc, carry_dec = (zero_enc, zero_dec)
    kept_enc = jnp.zeros((MICRO, MBUF, BUF, D), jnp.bfloat16)
    kept_dec = jnp.zeros((MICRO, MBUF, dec_rows, D), jnp.bfloat16)
    for step_id in range(MICRO + 3):
        micro_id = step_id - section_id
        active = (micro_id >= 0) & (micro_id < MICRO)
        slot_id = jnp.clip(micro_id, 0, MICRO - 1)
        kept_enc = kept_enc.at[slot_id].set(jnp.where(active, carry_enc, kept_enc[slot_id]))
        kept_dec = kept_dec.at[slot_id].set(jnp.where(active, carry_dec, kept_dec[slot_id]))
        if step_id < MICRO + 2:
            branch_id = jnp.where(active, section_id, 3)
            send_enc, send_dec = lax.switch(
                branch_id,
                (forward_zero, forward_one, forward_two, forward_three),
                carry_enc,
                carry_dec,
                slot_id,
            )
            carry_enc, carry_dec = (
                from_behind(for_sending(send_enc), "section", 1).astype(send_enc.dtype),
                from_behind(for_sending(send_dec), "section", 1).astype(send_dec.dtype),
            )
    grad_enc, grad_dec = (zero_enc, zero_dec)
    input_grads = jnp.zeros((MICRO, MBUF, BUF, D), jnp.bfloat16)
    output_rows = jnp.zeros((MICRO, MBUF, dec_rows, D), jnp.bfloat16)
    decoder_grads = jnp.zeros((MICRO, MBUF, dec_rows, D), jnp.bfloat16)
    blocks_total = zero_blocks
    gains_total = zero_gains
    tables_total = zero_tables
    for step_id in range(MICRO + 3):
        micro_id = step_id + section_id - 3
        active = (micro_id >= 0) & (micro_id < MICRO)
        slot_id = jnp.clip(micro_id, 0, MICRO - 1)
        branch_id = jnp.where(active, section_id, 4)
        results = lax.switch(
            branch_id,
            (backward_zero, backward_one, backward_two, backward_three, backward_nothing),
            kept_enc[slot_id],
            kept_dec[slot_id],
            grad_enc,
            grad_dec,
            slot_id,
        )
        (
            send_enc,
            send_dec,
            result_enc,
            result_out,
            result_dec,
            blocks_grad,
            gains_grad,
            tables_grad,
        ) = results
        blocks_total = blocks_total + jnp.where(active, blocks_grad, 0.0)
        gains_total = gains_total + jnp.where(active, gains_grad, 0.0)
        tables_total = tables_total + jnp.where(active, tables_grad, 0.0)
        input_grads = input_grads.at[slot_id].set(
            jnp.where(active, result_enc, input_grads[slot_id])
        )
        output_rows = output_rows.at[slot_id].set(
            jnp.where(active, result_out, output_rows[slot_id])
        )
        decoder_grads = decoder_grads.at[slot_id].set(
            jnp.where(active, result_dec, decoder_grads[slot_id])
        )
        if step_id < MICRO + 2:
            grad_enc, grad_dec = (
                from_behind(for_sending(send_enc), "section", -1).astype(send_enc.dtype),
                from_behind(for_sending(send_dec), "section", -1).astype(send_dec.dtype),
            )
    input_part, output_part, decoder_part = (
        lax.psum_scatter(
            input_grads.reshape(-1, BUF, D).astype(jnp.float32).astype(jnp.bfloat16),
            "section",
            scatter_dimension=1,
            tiled=True,
        ).astype(jnp.float32),
        lax.psum_scatter(
            output_rows.reshape(-1, dec_rows, D).astype(jnp.float32).astype(jnp.bfloat16),
            "section",
            scatter_dimension=1,
            tiled=True,
        ).astype(jnp.float32),
        lax.psum_scatter(
            decoder_grads.reshape(-1, dec_rows, D).astype(jnp.float32).astype(jnp.bfloat16),
            "section",
            scatter_dimension=1,
            tiled=True,
        ).astype(jnp.float32),
    )
    summed = lax.psum(blocks_total, "dp")
    home = lax.all_to_all(
        summed[None].astype(jnp.bfloat16), "section", split_axis=2, concat_axis=0, tiled=True
    ).astype(jnp.float32)
    query_grad, keyval_grad, output_grad, feed_in_grad, feed_out_grad = unpack_home(home)
    gains_sum, tables_sum = lax.psum((gains_total, tables_total), ("dp", "section"))
    return (
        output_part.astype(jnp.bfloat16),
        input_part.astype(jnp.bfloat16),
        decoder_part.astype(jnp.bfloat16),
        query_grad,
        keyval_grad,
        output_grad,
        feed_in_grad,
        feed_out_grad,
        gains_sum,
        tables_sum,
    )


def solution(mesh):
    return jax.shard_map(
        shards,
        mesh=mesh,
        in_specs=(
            P("dp", None, None),
            P("dp", None, None),
            P("dp", None),
            P("dp", None),
            P(None, "section", None),
            P(None, "section", None),
            P(None, "section", None),
            P(None, "section", None),
            P(None, "section", None),
            P(),
            P(),
            P("dp", None, None),
        ),
        out_specs=(
            P("dp", "section", None),
            P("dp", "section", None),
            P("dp", "section", None),
            P(None, "section", None),
            P(None, "section", None),
            P(None, "section", None),
            P(None, "section", None),
            P(None, "section", None),
            P(),
            P(),
        ),
        check_vma=False,
    )
```

profile of v0, /device:TPU:0, one launch (start us, length us, event | category | flops | bytes accessed | tf_op | source)
XLA Modules:
  0.0 5719.1 jit_solution(15588317195042731601)
XLA Ops:
  23.3 105.0 %all-to-all-done = bf16[4,8,192,768]{3,2,1,0:T(8,128)(2,1)} async-done(((bf16[4,8,192,768]{3,2,1,0:T(8,128)(2,1)}), bf16[4,8,192,768]{3,2,1,0:T(8,128)(2,1)}, u32[]{:S(2)}, u32[]{:S(2)}) %all-to-all-start) | async-done | bytes 9437216 | tf_op jit(solution)/shard_map/all_to_all | solution.py:460
  136.9 991.2 %conditional.9 = (bf16[1,512,768]{2,1,0:T(8,128)(2,1)}, bf16[1,96,768]{2,1,0:T(8,128)(2,1)}) conditional(s32[]{:T(128)} %clamp.57, (s32[]{:T(128)}, bf16[2,512,768]{2,1,0:T(8,128)(2,1)S(1)}, f32[5,768]{1,0:T(8,128)S(1)}, bf16[8,768,768]{2,1,0:T(8,128)(2,1)}, s32[2,3]{1,0:T(2,128)S(1)}, ...), branch_computations={%region_2.9_spmd, %region_8.10_spmd, %region_9.21_spmd, %region_19... | conditional | flops 4846388736 | bytes 132361376 | solution.py:604
  141.4 860.1 %gather_fusion.10 = f32[262144,12]{1,0:T(8,128)} fusion(f32[12,32]{0,1:T(8,128)S(1)} %slice_bitcast_fusion, s32[262144]{0:T(1024)S(1)} %broadcast_clamp_fusion), kind=kCustom, calls=%fused_computation.clone | custom fusion | bytes 26214400 | tf_op jit(solution)/shard_map/cond/branch_0_fun/jit(_take)/gather | solution.py:78
  1001.6 73.5 %copy.901 = f32[512,512,12]{0,1,2:T(8,128)} copy(f32[512,512,12]{2,1,0:T(8,128)} %bitcast.11) | data formatting | bytes 25165824 | tf_op jit(solution)/shard_map/cond/branch_0_fun/jit(_take)/gather | solution.py:78
  1104.0 12.1 fusion.378
  1135.4 1086.9 %conditional.10 = (bf16[1,512,768]{2,1,0:T(8,128)(2,1)}, bf16[1,96,768]{2,1,0:T(8,128)(2,1)}) conditional(s32[]{:T(128)} %clamp.58, (s32[]{:T(128)}, bf16[2,512,768]{2,1,0:T(8,128)(2,1)S(1)}, f32[5,768]{1,0:T(8,128)S(1)}, bf16[8,768,768]{2,1,0:T(8,128)(2,1)}, s32[2,3]{1,0:T(2,128)S(1)}, ...), branch_computations={%region_21.29_spmd, %region_27.31_spmd, %region_29.41_spmd, %regio... | conditional | flops 4849926656 | bytes 129215616 | solution.py:604
  1142.9 943.3 %gather_fusion.12 = f32[262144,12]{1,0:T(8,128)} fusion(f32[12,32]{0,1:T(8,128)S(1)} %slice_bitcast_fusion.2, s32[262144]{0:T(1024)} %broadcast_clamp_fusion.2), kind=kCustom, calls=%fused_computation.2.clone | custom fusion | bytes 26214400 | tf_op jit(solution)/shard_map/cond/branch_0_fun/jit(_take)/gather | solution.py:78
  2086.2 73.6 %copy.919 = f32[512,512,12]{0,1,2:T(8,128)} copy(f32[512,512,12]{2,1,0:T(8,128)} %bitcast.58) | data formatting | bytes 25165824 | tf_op jit(solution)/shard_map/cond/branch_0_fun/jit(_take)/gather | solution.py:78
  2174.9 12.6 fusion.493
  2197.8 12.4 fusion.501
  2242.8 11.7 collective-permute-start.2
  2278.0 84.5 %collective-permute-start.7 = (bf16[1,96,768]{2,1,0:T(8,128)(2,1)}, bf16[1,96,768]{2,1,0:T(8,128)(2,1)S(1)}, u32[]{:S(2)}, u32[]{:S(2)}) collective-permute-start(bf16[1,96,768]{2,1,0:T(8,128)(2,1)} %get-tuple-element.2402), channel_id=1, source_target_pairs={{0,1},{1,2},{2,3},{4,5},{5,6},{6,7},{8,9},{9,10},{10,11},{12,13},{... | collective-permute-start | bytes 442376 | tf_op jit(solution)/shard_map/ppermute | solution.py:32
  2369.0 43.4 conditional.13
  2420.9 43.5 conditional.14
  2467.0 13.1 collective-permute-done.11
  2481.0 43.6 conditional.15
  2527.3 234.7 %collective-permute-done.13 = bf16[1,96,768]{2,1,0:T(8,128)(2,1)S(1)} collective-permute-done((bf16[1,96,768]{2,1,0:T(8,128)(2,1)}, bf16[1,96,768]{2,1,0:T(8,128)(2,1)S(1)}, u32[]{:S(2)}, u32[]{:S(2)}) %collective-permute-start.13) | collective-permute-done | bytes 147488 | tf_op jit(solution)/shard_map/ppermute | solution.py:32
  2762.0 1178.8 %conditional.16 = (bf16[1,512,768]{2,1,0:T(8,128)(2,1)}, bf16[1,96,768]{2,1,0:T(8,128)(2,1)}, bf16[1,512,768]{2,1,0:T(8,128)(2,1)}, bf16[1,96,768]{2,1,0:T(8,128...) conditional(s32[]{:T(128)} %clamp.63, (s32[]{:T(128)}, ...), branch_computations={%region_185.196_spmd, %region_194.200_spmd, %region_198.216_spmd, ... | conditional | flops 12160993280 | bytes 434145024 | solution.py:627
  2767.7 943.3 %gather_fusion.6 = f32[262144,12]{1,0:T(8,128)} fusion(f32[12,32]{0,1:T(8,128)S(1)} %slice_bitcast_fusion.14, s32[262144]{0:T(1024)} %broadcast_clamp_fusion.14), kind=kCustom, calls=%fused_computation.8.clone | custom fusion | bytes 26214400 | tf_op jit(solution)/shard_map/cond/branch_0_fun/jit(_take)/gather | solution.py:78
  3711.0 73.4 %copy.1071 = f32[512,512,12]{0,1,2:T(8,128)} copy(f32[512,512,12]{2,1,0:T(8,128)} %bitcast.529) | data formatting | bytes 25165824 | tf_op jit(solution)/shard_map/cond/branch_0_fun/jit(_take)/gather | solution.py:78
  3813.7 10.6 multiply_reduce_fusion.22
  3865.3 24.7 copy.1310
  3891.7 11.5 fusion.1490
  3946.3 1166.2 %conditional.17 = (bf16[1,512,768]{2,1,0:T(8,128)(2,1)S(1)}, bf16[1,96,768]{2,1,0:T(8,128)(2,1)S(1)}, bf16[1,96,768]{2,1,0:T(8,128)(2,1)}, f32[5,768]{1,0:T(8,12...) conditional(s32[]{:T(128)} %clamp.64, (s32[]{:T(128)}, ...), branch_computations={%region_220.231_spmd, %region_229.234_spmd, %region_232.250_spmd, ... | conditional | flops 12156272640 | bytes 439445120 | solution.py:627
  3953.7 943.3 %gather_fusion.8 = f32[262144,12]{1,0:T(8,128)} fusion(f32[12,32]{0,1:T(8,128)S(1)} %slice_bitcast_fusion.16, s32[262144]{0:T(1024)} %broadcast_clamp_fusion.16), kind=kCustom, calls=%fused_computation.9.clone | custom fusion | bytes 26214400 | tf_op jit(solution)/shard_map/cond/branch_0_fun/jit(_take)/gather | solution.py:78
  4897.0 73.4 %copy.1104 = f32[512,512,12]{0,1,2:T(8,128)} copy(f32[512,512,12]{2,1,0:T(8,128)} %bitcast.638) | data formatting | bytes 25165824 | tf_op jit(solution)/shard_map/cond/branch_0_fun/jit(_take)/gather | solution.py:78
  5047.2 25.0 copy.1320
  5072.9 12.0 fusion.1689
  5112.5 21.2 select_add_fusion.5
  5133.8 372.6 %all-reduce.32 = bf16[8,768,768]{2,0,1:T(8,128)(2,1)} all-reduce(f32[8,768,768]{2,0,1:T(8,128)} %select_add_fusion.5), channel_id=1, replica_groups=mesh['dp'=8,'section'=4] {'dp'}, use_global_device_ids=true, to_apply=%region_255.258 | all-reduce | flops 4718592 | bytes 28311552 | tf_op jit(solution)/shard_map/psum | solution.py:683
  5533.1 128.2 %all-reduce.30 = (f32[5,768]{1,0:T(8,128)}, f32[2,32,12]{1,0,2:T(2,128)}) all-reduce(f32[5,768]{1,0:T(8,128)S(1)} %select_add_fusion.6, f32[2,32,12]{1,0,2:T(2,128)S(1)} %select_add_fusion.7), channel_id=1, replica_groups=mesh['dp'=8,'section'=4] {'dp','section'}, use_global_device_ids=true, to_apply=%region_256.259 | all-reduce | flops 4608 | bytes 36864 | tf_op jit(solution)/shard_map/psum | solution.py:688
  5673.7 12.6 convert_bitcast_fusion.31
  (451 shorter events, 445.9 us)
Async XLA Ops:
  17.4 110.9 %all-to-all-start = ((bf16[4,8,192,768]{3,2,1,0:T(8,128)(2,1)}), bf16[4,8,192,768]{3,2,1,0:T(8,128)(2,1)}, u32[]{:S(2)}, u32[]{:S(2)}) async-start(bf16[4,8,192,768]{3,2,1,0:T(8,128)(2,1)} %pad_maximum_fusion.10), calls=%async_computation | async-start | bytes 18874368 | tf_op jit(solution)/shard_map/all_to_all | solution.py:460
  136.9 993.4 %copy-start.352 = (s32[4]{0:T(128)S(1)}, s32[4]{0:T(128)}, u32[]{:S(2)}) copy-start(s32[4]{0:T(128)} %constant.3705.clone.1) | copy-start | bytes 52
  1128.0 7.4 collective-permute-start
  1133.5 1091.9 %collective-permute-start.4 = (bf16[1,96,768]{2,1,0:T(8,128)(2,1)}, bf16[1,96,768]{2,1,0:T(8,128)(2,1)}, u32[]{:S(2)}, u32[]{:S(2)}) collective-permute-start(bf16[1,96,768]{2,1,0:T(8,128)(2,1)} %get-tuple-element.2399), channel_id=1, source_target_pairs={{0,1},{1,2},{2,3},{4,5},{5,6},{6,7},{8,9},{9,10},{10,11},{12,13},{... | collective-permute-start | bytes 442376 | tf_op jit(solution)/shard_map/ppermute | solution.py:32
  2222.3 10.9 collective-permute-start.1
  2229.2 25.3 collective-permute-start.5
  2242.8 19.5 collective-permute-start.2
  2258.4 16.4 collective-permute-start.6
  2272.3 93.8 %collective-permute-start.3 = (bf16[1,512,768]{2,1,0:T(8,128)(2,1)}, bf16[1,512,768]{2,1,0:T(8,128)(2,1)S(1)}, u32[]{:S(2)}, u32[]{:S(2)}) collective-permute-start(bf16[1,512,768]{2,1,0:T(8,128)(2,1)} %get-tuple-element.2398), channel_id=1, source_target_pairs={{0,1},{1,2},{2,3},{4,5},{5,6},{6,7},{8,9},{9,10},{10,11},{12,13},{... | collective-permute-start | bytes 2359304 | tf_op jit(solution)/shard_map/ppermute | solution.py:32
  2277.0 87.6 %copy-start.28 = (bf16[2,1,96,768]{3,2,1,0:T(8,128)(2,1)S(1)}, bf16[2,1,96,768]{3,2,1,0:T(8,128)(2,1)}, u32[]{:S(2)}) copy-start(bf16[2,1,96,768]{3,2,1,0:T(8,128)(2,1)} %fusion.2237) | copy-start | bytes 884740
  2278.0 86.6 %collective-permute-start.7 = (bf16[1,96,768]{2,1,0:T(8,128)(2,1)}, bf16[1,96,768]{2,1,0:T(8,128)(2,1)S(1)}, u32[]{:S(2)}, u32[]{:S(2)}) collective-permute-start(bf16[1,96,768]{2,1,0:T(8,128)(2,1)} %get-tuple-element.2402), channel_id=1, source_target_pairs={{0,1},{1,2},{2,3},{4,5},{5,6},{6,7},{8,9},{9,10},{10,11},{12,13},{... | collective-permute-start | bytes 442376 | tf_op jit(solution)/shard_map/ppermute | solution.py:32
  2369.0 51.8 copy-start.38
  2412.5 8.4 collective-permute-start.8
  2413.8 7.1 collective-permute-start.9
  2464.4 16.7 copy-start.305
  2464.4 15.7 collective-permute-start.10
  2465.7 14.4 collective-permute-start.11
  2481.0 281.0 %copy-start.35 = (bf16[1,1,512,768]{3,2,1,0:T(8,128)(2,1)S(1)}, bf16[1,1,512,768]{3,2,1,0:T(8,128)(2,1)}, u32[]{:S(2)}) copy-start(bf16[1,1,512,768]{3,2,1,0:T(8,128)(2,1)} %get-tuple-element.3371) | copy-start | bytes 2359300
  2524.7 237.4 %copy-start.307 = (f32[2,32,12]{1,0,2:T(2,128)}, f32[2,32,12]{1,0,2:T(2,128)S(1)}, u32[]{:S(2)}) copy-start(f32[2,32,12]{1,0,2:T(2,128)S(1)} %get-tuple-element.3058) | copy-start | bytes 9220
  2524.7 237.3 %collective-permute-start.12 = (bf16[1,512,768]{2,1,0:T(8,128)(2,1)}, bf16[1,512,768]{2,1,0:T(8,128)(2,1)}, u32[]{:S(2)}, u32[]{:S(2)}) collective-permute-start(bf16[1,512,768]{2,1,0:T(8,128)(2,1)} %get-tuple-element.2410), channel_id=1, source_target_pairs={{1,0},{2,1},{3,2},{5,4},{6,5},{7,6},{9,8},{10,9},{11,10},{13,12},{... | collective-permute-start | bytes 2359304 | tf_op jit(solution)/shard_map/ppermute | solution.py:32
  2526.0 236.0 %collective-permute-start.13 = (bf16[1,96,768]{2,1,0:T(8,128)(2,1)}, bf16[1,96,768]{2,1,0:T(8,128)(2,1)S(1)}, u32[]{:S(2)}, u32[]{:S(2)}) collective-permute-start(bf16[1,96,768]{2,1,0:T(8,128)(2,1)} %get-tuple-element.2411), channel_id=1, source_target_pairs={{1,0},{2,1},{3,2},{5,4},{6,5},{7,6},{9,8},{10,9},{11,10},{13,12},{... | collective-permute-start | bytes 442376 | tf_op jit(solution)/shard_map/ppermute | solution.py:32
  2762.3 1027.0 %copy-start.301 = (f32[512]{0:T(512)}, f32[512]{0:T(512)S(1)}, u32[]{:S(2)}) copy-start(f32[512]{0:T(512)S(1)} %fusion.1514) | copy-start | bytes 6148 | tf_op jit(solution)/shard_map/cond
  2763.1 1026.3 %copy-start.272 = (f32[768]{0:T(1024)}, f32[768]{0:T(1024)S(1)}, u32[]{:S(2)}) copy-start(f32[768]{0:T(1024)S(1)} %slice_reduce_fusion.29) | copy-start | bytes 9220 | tf_op jit(solution)/shard_map/cond
  3940.9 5.4 collective-permute-start.14
  3942.2 4.1 collective-permute-start.15
  5112.5 21.3 copy-start.92
  5112.5 21.3 copy-start.245
  5112.5 21.3 copy-start.311
  5506.3 158.1 %all-to-all-start.1 = ((bf16[1,8,768,768]{3,1,0,2:T(8,128)(2,1)}), bf16[1,8,768,768]{3,1,0,2:T(8,128)(2,1)}, u32[]{:S(2)}, u32[]{:S(2)}) async-start(bf16[1,8,768,768]{3,1,0,2:T(8,128)(2,1)} %bitcast.3502), calls=%async_computation.2 | async-start | bytes 18874368 | tf_op jit(solution)/shard_map/all_to_all | solution.py:684
  5512.3 149.0 %reduce-scatter.10.cloned.1.call-start = ((), (), s32[]{:S(2)}) async-start(), calls=%async_computation.6 | async-start | bytes 368640
  5523.2 139.6 %reduce-scatter.12.cloned.1.call-start = ((), (), s32[]{:S(2)}) async-start(), calls=%async_computation.7 | async-start | bytes 368640
  5528.3 184.0 %reduce-scatter.8.cloned.1.call-start = ((), (), s32[]{:S(2)}) async-start(), calls=%async_computation.5 | async-start | bytes 1966080 | tf_op jit(solution)/shard_map/reduce_scatter | solution.py:664
  (59 other events, 262.1 us)
Sparse Core Ops, SparseCore 0:
  5523.3 25.4 reduce-scatter.9
  5552.0 21.9 reduce-scatter.11
  5577.0 36.7 reduce-scatter.7
where the time goes:
time: 5790 us; the launch traced here: 5720 us
  local copies, waits for them, and re-layouts  4190 us (72%)
  blocking collectives  501 us (9%)
  waiting for transfers between devices  362 us (6%)
  matrix products  200 us (3%)
  loops' own time  189 us (3%)
  other arithmetic  134 us (2%)
  starting transfers between devices  131 us (2%)
    gather x8, local copies, waits for them, and re-layouts, full_bias(): return jnp.take(jnp.transpose(table), bucket, axis=1)  3980 us
    psum x1, blocking collectives, shards(): summed = lax.psum(blocks_total, 'dp')  373 us
    ppermute x16, waiting for transfers between devices, from_behind(): lax.ppermute(value, axis, [(source, source + steps) for source in range(f...  256 us
    another operation x5, loops' own time, shards(): lax.switch(branch_id, (backward_zero, backward_one, backward_two, backwar...  156 us
    psum x1, blocking collectives, shards(): lax.psum((gains_total, tables_total), ('dp', 'section'))  128 us
    ppermute x16, starting transfers between devices, from_behind(): lax.ppermute(value, axis, [(source, source + steps) for source in range(f...  119 us
  transfers between devices with their start and end apart: 21, of which 5 were waited for; matrix products, arithmetic and copies ran while one was open for 21% of the time, Pallas kernels for 0%

commit v1 on v0

v1 whole, which is shorter than its diff:
```python
import functools

import jax
import jax.numpy as jnp
import numpy as np
from jax import lax
from jax.experimental import pallas as pl
from jax.experimental.pallas import tpu as pltpu
from jax.sharding import PartitionSpec as P

D = 768
HEADS = 12
HD = 64
PAIRS = HEADS // 2
NB = 32
BUF = 512
BIG = 384
SMALL = 64
REST = BUF - BIG
QPB = 3
TGT = 32
DEC = QPB * TGT
WIDE = 512
epsilon = 1e-06
masked_score = -1e30
enc_edges = (12, 16, 23, 32, 46, 64, 91)
dec_edges = (19, 21, 24, 27, 31)
bf16 = jnp.bfloat16
f32 = jnp.float32


def dot_nn(a, b):
    return lax.dot_general(a, b, (((1,), (0,)), ((), ())), preferred_element_type=f32)


def dot_nt(a, b):
    return lax.dot_general(a, b, (((1,), (1,)), ((), ())), preferred_element_type=f32)


def dot_tn(a, b):
    return lax.dot_general(a, b, (((0,), (0,)), ((), ())), preferred_element_type=f32)


def encoder_bucket(offset):
    distance = np.abs(offset)
    bucket = np.minimum(distance, 8)
    for boundary in enc_edges:
        bucket = bucket + (distance >= boundary)
    return bucket + 16 * (offset > 0)


def decoder_bucket(offset):
    distance = np.maximum(-offset, 0)
    bucket = np.minimum(distance, 16)
    for boundary in dec_edges:
        bucket = bucket + (distance >= boundary)
    return bucket


def enc_offsets():
    lane = np.arange(WIDE)
    shifted = np.where(lane < BIG, lane, lane - WIDE)
    return 128 * np.arange(3)[:, None] - shifted[None, :]


def diagonal_offsets(rows, width):
    return rows - 1 - np.arange(width)


def dec_offsets():
    lane = np.arange(256)
    return -np.where(lane < 128, lane, lane - 256)


def one_hot(bucket):
    return (bucket[..., None] == np.arange(NB)).astype(np.float32)


def spread_table(table, bucket):
    hot = jnp.asarray(one_hot(bucket))
    return jnp.sum(hot[None] * jnp.transpose(table).reshape((HEADS,) + (1,) * bucket.ndim + (NB,)), axis=-1)


def lane_half(value, which):
    lane = lax.broadcasted_iota(jnp.int32, value.shape, 1)
    keep = (lane < HD) if which == 0 else (lane >= HD)
    return jnp.where(keep, value, jnp.zeros_like(value))


def softmax_t(scores):
    peak = jnp.max(scores, axis=0, keepdims=True)
    raised = jnp.exp(scores - peak)
    total = jnp.sum(raised, axis=0, keepdims=True)
    return (raised * (1.0 / total)).astype(bf16)


def toeplitz(row, rows):
    spread = jnp.broadcast_to(row, (rows, row.shape[-1]))
    return pltpu.roll(spread, 0, 1, stride=1, stride_axis=0)


def diagonals(value, width):
    rows = value.shape[0]
    row = lax.broadcasted_iota(jnp.int32, (rows, rows), 0)
    col = lax.broadcasted_iota(jnp.int32, (rows, rows), 1)
    flipped = dot_nn((row + col == rows - 1).astype(bf16), value)
    padded = jnp.concatenate([flipped, jnp.zeros((rows, width - value.shape[1]), f32)], axis=1)
    return jnp.sum(pltpu.roll(padded, 0, 1, stride=1, stride_axis=0), axis=0, keepdims=True)


def rest_mask():
    row = lax.broadcasted_iota(jnp.int32, (REST, REST), 0) // SMALL
    col = lax.broadcasted_iota(jnp.int32, (REST, REST), 1) // SMALL
    return row == col


def enc_forward_kernel(q_ref, k_ref, v_ref, bias_ref, c_ref, big_ref, rest_ref):
    values_t = v_ref[...].T
    keys = k_ref[...]
    allowed = rest_mask()
    heads = []
    for hh in range(2):
        queries = lane_half(q_ref[...], hh)
        bias = [toeplitz(bias_ref[hh, b : b + 1, :], 128)[:, :BIG] for b in range(3)]
        scores = dot_nt(keys[:BIG], queries[:BIG]) + jnp.concatenate(bias, axis=0)
        weights = softmax_t(scores)
        big_ref[hh] = weights
        head_v = values_t[hh * HD : (hh + 1) * HD]
        context = dot_nn(head_v[:, :BIG], weights)
        rest = dot_nt(keys[BIG:], queries[BIG:]) + bias[0][:, :REST]
        rest = softmax_t(jnp.where(allowed, rest, masked_score))
        rest_ref[hh] = rest
        heads.append(jnp.concatenate([context, dot_nn(head_v[:, BIG:], rest)], axis=1))
    c_ref[...] = jnp.concatenate(heads, axis=0).T.astype(bf16)


def score_grad(weights, grad_weights, row_sum):
    return (weights.astype(f32) * (grad_weights - row_sum)).astype(bf16)


def enc_backward_kernel(
    q_ref, k_ref, v_ref, c_ref, g_ref, big_ref, rest_ref,
    dq_ref, dk_ref, dv_ref, diag_ref, rdiag_ref,
):
    grads = g_ref[...]
    keys_t = k_ref[...].T
    product_t = (grads.astype(f32) * c_ref[...].astype(f32)).T
    dq_t = []
    dk_big = dv_big = dk_rest = dv_rest = 0.0
    for hh in range(2):
        row_sum = jnp.sum(product_t[hh * HD : (hh + 1) * HD], axis=0, keepdims=True)
        queries = lane_half(q_ref[...], hh)
        values = lane_half(v_ref[...], hh)
        grads_h = lane_half(grads, hh)
        head_k = keys_t[hh * HD : (hh + 1) * HD]
        weights = big_ref[hh]
        ds = score_grad(weights, dot_nt(values[:BIG], grads[:BIG]), row_sum[:, :BIG])
        dv_big = dv_big + dot_nn(weights, grads_h[:BIG])
        dk_big = dk_big + dot_nn(ds, queries[:BIG])
        diag_ref[hh] = jnp.concatenate(
            [diagonals(ds[128 * b : 128 * (b + 1)], WIDE) for b in range(3)], axis=0
        )
        dq_head = dot_nn(head_k[:, :BIG], ds)
        weights = rest_ref[hh]
        ds = score_grad(weights, dot_nt(values[BIG:], grads[BIG:]), row_sum[:, BIG:])
        dv_rest = dv_rest + dot_nn(weights, grads_h[BIG:])
        dk_rest = dk_rest + dot_nn(ds, queries[BIG:])
        rdiag_ref[hh] = diagonals(ds, 2 * REST)
        dq_t.append(jnp.concatenate([dq_head, dot_nn(head_k[:, BIG:], ds)], axis=1))
    dq_ref[...] = jnp.concatenate(dq_t, axis=0).T.astype(bf16)
    dk_ref[...] = jnp.concatenate([dk_big, dk_rest], axis=0).astype(bf16)
    dv_ref[...] = jnp.concatenate([dv_big, dv_rest], axis=0).astype(bf16)


def pair_spec(rows):
    return pl.BlockSpec((rows, 2 * HD), lambda p: (0, p))


def head_spec(*dims):
    return pl.BlockSpec((2,) + dims, lambda p: (p,) + (0,) * len(dims))


def call(kernel, outs, in_specs, out_specs, flops, *args):
    return pl.pallas_call(
        kernel,
        grid=(PAIRS,),
        out_shape=outs,
        in_specs=in_specs,
        out_specs=out_specs,
        compiler_params=pltpu.CompilerParams(vmem_limit_bytes=40 << 20),
        cost_estimate=pl.CostEstimate(flops=flops, bytes_accessed=8 << 20, transcendentals=0),
    )(*args)


def shape(dims, dtype=bf16):
    return jax.ShapeDtypeStruct(dims, dtype)


def enc_attend(q, k, v, bias):
    return call(
        enc_forward_kernel,
        (shape((BUF, D)), shape((HEADS, BIG, BIG)), shape((HEADS, REST, REST))),
        [pair_spec(BUF)] * 3 + [head_spec(3, WIDE)],
        (pair_spec(BUF), head_spec(BIG, BIG), head_spec(REST, REST)),
        4_000_000_000,
        q, k, v, bias,
    )


def enc_attend_back(q, k, v, c, g, big, rest):
    return call(
        enc_backward_kernel,
        (
            shape((BUF, D)), shape((BUF, D)), shape((BUF, D)),
            shape((HEADS, 3, WIDE), f32), shape((HEADS, 1, 2 * REST), f32),
        ),
        [pair_spec(BUF)] * 5 + [head_spec(BIG, BIG), head_spec(REST, REST)],
        (pair_spec(BUF),) * 3 + (head_spec(3, WIDE), head_spec(1, 2 * REST)),
        9_000_000_000,
        q, k, v, c, g, big, rest,
    )


def small_forward_kernel(kind, *refs):
    if kind == "self":
        q_ref, k_ref, v_ref, bias_ref, c_ref, p_ref = refs
    else:
        q_ref, k_ref, v_ref, c_ref, p_ref = refs
    keys = k_ref[...]
    values_t = v_ref[...].T
    count = keys.shape[0]
    row = lax.broadcasted_iota(jnp.int32, (count, DEC), 0)
    col = lax.broadcasted_iota(jnp.int32, (count, DEC), 1)
    if kind == "self":
        allowed = (row // TGT == col // TGT) & (row <= col)
    else:
        allowed = jnp.where(row < BIG, 0, row // SMALL - (BIG // SMALL - 1)) == col // TGT
    heads = []
    for hh in range(2):
        scores = dot_nt(keys, lane_half(q_ref[...], hh))
        if kind == "self":
            scores = scores + toeplitz(bias_ref[hh], DEC)[:, :DEC]
        weights = softmax_t(jnp.where(allowed, scores, masked_score))
        p_ref[hh] = weights
        heads.append(dot_nn(values_t[hh * HD : (hh + 1) * HD], weights))
    c_ref[...] = jnp.concatenate(heads, axis=0).T.astype(bf16)


def small_backward_kernel(kind, *refs):
    if kind == "self":
        q_ref, k_ref, v_ref, c_ref, g_ref, p_ref, dq_ref, dk_ref, dv_ref, diag_ref = refs
    else:
        q_ref, k_ref, v_ref, c_ref, g_ref, p_ref, dq_ref, dk_ref, dv_ref = refs
    grads = g_ref[...]
    keys_t = k_ref[...].T
    product_t = (grads.astype(f32) * c_ref[...].astype(f32)).T
    dq_t = []
    dk = dv = 0.0
    for hh in range(2):
        row_sum = jnp.sum(product_t[hh * HD : (hh + 1) * HD], axis=0, keepdims=True)
        weights = p_ref[hh]
        ds = score_grad(weights, dot_nt(lane_half(v_ref[...], hh), grads), row_sum)
        dv = dv + dot_nn(weights, lane_half(grads, hh))
        dk = dk + dot_nn(ds, lane_half(q_ref[...], hh))
        if kind == "self":
            diag_ref[hh] = diagonals(ds, 256)
        dq_t.append(dot_nn(keys_t[hh * HD : (hh + 1) * HD], ds))
    dq_ref[...] = jnp.concatenate(dq_t, axis=0).T.astype(bf16)
    dk_ref[...] = dk.astype(bf16)
    dv_ref[...] = dv.astype(bf16)


def small_attend(kind, q, k, v, bias=None):
    count = k.shape[0]
    specs = [pair_spec(DEC), pair_spec(count), pair_spec(count)]
    args = (q, k, v)
    if kind == "self":
        specs, args = specs + [head_spec(1, 256)], args + (bias,)
    return call(
        functools.partial(small_forward_kernel, kind),
        (shape((DEC, D)), shape((HEADS, count, DEC))),
        specs,
        (pair_spec(DEC), head_spec(count, DEC)),
        2_000_000_000,
        *args,
    )


def small_attend_back(kind, q, k, v, c, g, weights):
    count = k.shape[0]
    outs = (shape((DEC, D)), shape((count, D)), shape((count, D)))
    out_specs = (pair_spec(DEC), pair_spec(count), pair_spec(count))
    if kind == "self":
        outs, out_specs = outs + (shape((HEADS, 1, 256), f32),), out_specs + (head_spec(1, 256),)
    return call(
        functools.partial(small_backward_kernel, kind),
        outs,
        [pair_spec(DEC), pair_spec(count), pair_spec(count), pair_spec(DEC), pair_spec(DEC), head_spec(count, DEC)],
        out_specs,
        3_000_000_000,
        q, k, v, c, g, weights,
    )


def norm_scale(rows):
    return lax.rsqrt(jnp.mean(rows * rows, axis=-1, keepdims=True) + epsilon)


def norm_rows(rows, gain):
    return (rows * norm_scale(rows) * gain).astype(bf16)


def norm_back(rows, gain, grad):
    scale = norm_scale(rows)
    unit = rows * scale
    weighted = grad * gain
    grad_rows = scale * (weighted - unit * jnp.mean(weighted * unit, axis=-1, keepdims=True))
    return grad_rows, jnp.sum(grad * unit, axis=0)


def gelu_both(u):
    root = np.float32(np.sqrt(2.0 / np.pi))
    cubic = np.float32(0.044715)
    bend = jnp.tanh(root * (u + cubic * u * u * u))
    value = 0.5 * u * (1.0 + bend)
    slope = 0.5 * (1.0 + bend) + 0.5 * u * (1.0 - bend * bend) * root * (1.0 + 3.0 * cubic * u * u)
    return value.astype(bf16), slope.astype(bf16)


def swap_section(value, bit):
    count = lax.axis_size("section")
    return lax.ppermute(value, "section", [(i, i ^ bit) for i in range(count)])


def swap_dp(value, bit):
    count = lax.axis_size("dp")
    return lax.ppermute(value, "dp", [(i, i ^ bit) for i in range(count)])


def add_low(a, b):
    return (a.astype(f32) + b.astype(f32)).astype(bf16)


def halves(value, bit):
    half = value.shape[0] // 2
    mine = (lax.axis_index("dp") // bit) % 2
    keep = lax.dynamic_slice_in_dim(value, mine * half, half, 0)
    send = lax.dynamic_slice_in_dim(value, (1 - mine) * half, half, 0)
    return keep, send


def rejoin(keep, other, bit):
    mine = (lax.axis_index("dp") // bit) % 2
    return jnp.where(mine == 0, jnp.concatenate([keep, other]), jnp.concatenate([other, keep]))


def sum_dp(value, order):
    count = lax.axis_size("dp")
    if count != 8:
        return lax.psum(value, "dp")
    for bit in order[:-1]:
        keep, send = halves(value, bit)
        value = add_low(keep, swap_dp(send, bit))
    value = add_low(value, swap_dp(value, order[-1]))
    for bit in order[:-1][::-1]:
        value = rejoin(value, swap_dp(value, bit), bit)
    return value


def core_sum(own, other):
    return add_low(own, swap_section(other.astype(bf16), 1))


def gather_mats(own, section_id):
    across = swap_section(own, 2)
    near = swap_section(own, 1)
    far = swap_section(across, 1)
    full = jnp.zeros((own.shape[0], 4 * own.shape[1], D), bf16)
    for piece, bit in ((own, 0), (near, 1), (across, 2), (far, 3)):
        full = lax.dynamic_update_slice_in_dim(full, piece, (section_id ^ bit) * own.shape[1], 1)
    return full


def shards(
    encoder_in, decoder_in, lengths, query_map, attn_query, attn_keyval, attn_output,
    feed_in, feed_out, norm_gains, position_bias, cotangent,
):
    section_id = lax.axis_index("section")
    across = section_id // 2
    core = section_id % 2
    quarter = attn_query.shape[1]
    half = 2 * quarter

    enc_w = gather_mats(jnp.concatenate([attn_query[0:1], attn_keyval[0:2], attn_output[0:1]]), section_id)
    self_w = gather_mats(jnp.concatenate([attn_query[1:2], attn_keyval[2:4], attn_output[1:2]]), section_id)
    cross_w = gather_mats(jnp.concatenate([attn_query[2:3], attn_keyval[4:6], attn_output[2:3]]), section_id)
    feed_in_o, feed_out_o = swap_section(feed_in, 1), swap_section(feed_out, 1)
    w_in = [jnp.concatenate([feed_in[i], feed_in_o[i]]) for i in range(2)]
    w_out = [jnp.concatenate([feed_out[i], feed_out_o[i]]) for i in range(2)]

    big = jnp.argmax(lengths[core]).astype(jnp.int32)
    start = big * SMALL
    owners = lax.dynamic_slice_in_dim(jnp.concatenate([query_map[core]] * 2), big, QPB, 0)

    def to_front(rows):
        return lax.dynamic_slice_in_dim(jnp.concatenate([rows, rows]), start, BUF, 0)

    def from_front(rows):
        return lax.dynamic_slice_in_dim(jnp.concatenate([rows, rows]), BUF - start, BUF, 0)

    def by_owner(rows):
        return jnp.concatenate(
            [lax.dynamic_slice_in_dim(rows, owners[i] * TGT, TGT, 0) for i in range(QPB)]
        )

    def from_owner(rows):
        whole = jnp.zeros((DEC, D), rows.dtype)
        for i in range(QPB):
            whole = lax.dynamic_update_slice_in_dim(whole, rows[i * TGT : (i + 1) * TGT], owners[i] * TGT, 0)
        return whole

    enc_rows = to_front(encoder_in[core]).astype(f32)
    dec_rows = by_owner(decoder_in[core]).astype(f32)
    cot = by_owner(cotangent[core])

    enc_table = spread_table(position_bias[0], encoder_bucket(enc_offsets()))
    dec_table = spread_table(position_bias[1], decoder_bucket(dec_offsets())[None])

    n1 = norm_rows(enc_rows, norm_gains[0])
    q1, k1, v1 = (dot_nn(n1, enc_w[i]).astype(bf16) for i in range(3))
    c1, p1_big, p1_rest = enc_attend(q1, k1, v1, enc_table)
    h1 = (enc_rows + dot_nn(c1, enc_w[3])).astype(bf16)
    h1_rows = h1.astype(f32)
    n2 = norm_rows(h1_rows, norm_gains[1])
    a1, slope1 = gelu_both(dot_nt(n2, w_in[0]))
    part = dot_nn(a1, w_out[0]).astype(bf16)
    e = (h1_rows + part.astype(f32) + swap_section(part, 2).astype(f32)).astype(bf16)

    n3 = norm_rows(dec_rows, norm_gains[2])
    q2, k2, v2 = (dot_nn(n3, self_w[i]).astype(bf16) for i in range(3))
    c2, p2 = small_attend("self", q2, k2, v2, dec_table)
    m = dec_rows + dot_nn(c2, self_w[3])
    n4 = norm_rows(m, norm_gains[3])
    q3 = dot_nn(n4, cross_w[0]).astype(bf16)
    k3 = dot_nn(e, cross_w[1]).astype(bf16)
    v3 = dot_nn(e, cross_w[2]).astype(bf16)
    c3, p3 = small_attend("cross", q3, k3, v3)
    g = (m + dot_nn(c3, cross_w[3])).astype(bf16)
    g_rows = g.astype(f32)
    n5 = norm_rows(g_rows, norm_gains[4])
    a2, slope2 = gelu_both(dot_nt(n5, w_in[1]))

    def feed_back(grad, a, slope, n, index):
        du = (slope.astype(f32) * dot_nt(grad, w_out[index])).astype(bf16)
        dn = dot_nn(du, w_in[index]).astype(bf16)
        dn = dn.astype(f32) + swap_section(dn, 2).astype(f32)
        dw_in = dot_tn(du, n)
        dw_out = dot_tn(a, grad)
        return dn, core_sum(dw_in[:D], dw_in[D:]), core_sum(dw_out[:D], dw_out[D:])

    dn5, unit_in2, unit_out2 = feed_back(cot, a2, slope2, n5, 1)
    unit_in2 = sum_dp(unit_in2, (1, 2, 4))
    unit_out2 = sum_dp(unit_out2, (2, 4, 1))
    part = dot_nn(a2, w_out[1]).astype(bf16)
    out_rows = g_rows + part.astype(f32) + swap_section(part, 2).astype(f32)
    dg_rows, gain4 = norm_back(g_rows, norm_gains[4], dn5)
    dg = (dg_rows + cot.astype(f32)).astype(bf16)

    def chip_cols(rows):
        return lax.dynamic_slice_in_dim(rows, across * half, half, 1)

    def unit_of(pairs):
        own, other = [], []
        for rows, grad in pairs:
            full = dot_tn(chip_cols(rows), grad).astype(bf16)
            own.append(lax.dynamic_slice_in_dim(full, core * quarter, quarter, 0))
            other.append(lax.dynamic_slice_in_dim(full, (1 - core) * quarter, quarter, 0))
        return core_sum(jnp.concatenate(own), jnp.concatenate(other))

    dc3 = dot_nt(dg, cross_w[3]).astype(bf16)
    dq3, dk3, dv3 = small_attend_back("cross", q3, k3, v3, c3, dc3, p3)
    de = (dot_nt(dk3, cross_w[1]) + dot_nt(dv3, cross_w[2])).astype(bf16)
    dm_rows, gain3 = norm_back(m, norm_gains[3], dot_nt(dq3, cross_w[0]))
    dm = dm_rows + dg.astype(f32)
    dm_low = dm.astype(bf16)
    unit_cross = sum_dp(unit_of([(n4, dq3), (e, dk3), (e, dv3), (c3, dg)]), (1, 2, 4))

    dn2, unit_in1, unit_out1 = feed_back(de, a1, slope1, n2, 0)
    unit_in1 = sum_dp(unit_in1, (1, 2, 4))
    unit_out1 = sum_dp(unit_out1, (2, 4, 1))
    dh1_rows, gain1 = norm_back(h1_rows, norm_gains[1], dn2)
    dh1 = (dh1_rows + de.astype(f32)).astype(bf16)

    dc2 = dot_nt(dm_low, self_w[3]).astype(bf16)
    dq2, dk2, dv2, diag2 = small_attend_back("self", q2, k2, v2, c2, dc2, p2)
    dn3 = dot_nt(dq2, self_w[0]) + dot_nt(dk2, self_w[1]) + dot_nt(dv2, self_w[2])
    dd_rows, gain2 = norm_back(dec_rows, norm_gains[2], dn3)
    dec_grad = dd_rows + dm
    unit_self = sum_dp(unit_of([(n3, dq2), (n3, dk2), (n3, dv2), (c2, dm_low)]), (1, 2, 4))

    dc1 = dot_nt(dh1, enc_w[3]).astype(bf16)
    dq1, dk1, dv1, diag1, rdiag1 = enc_attend_back(q1, k1, v1, c1, dc1, p1_big, p1_rest)
    unit_enc = sum_dp(unit_of([(n1, dq1), (n1, dk1), (n1, dv1), (c1, dh1)]), (1, 2, 4))
    dn1 = dot_nt(dq1, enc_w[0]) + dot_nt(dk1, enc_w[1]) + dot_nt(dv1, enc_w[2])
    de_rows, gain0 = norm_back(enc_rows, norm_gains[0], dn1)
    enc_grad = de_rows + dh1.astype(f32)

    hot_enc = jnp.asarray(
        np.concatenate(
            [one_hot(encoder_bucket(128 * b + diagonal_offsets(128, WIDE))) for b in range(3)]
            + [one_hot(encoder_bucket(diagonal_offsets(REST, 2 * REST)))]
        )
    )
    hot_dec = jnp.asarray(one_hot(decoder_bucket(diagonal_offsets(DEC, 256))))
    sums_enc = jnp.concatenate([diag1.reshape(HEADS, -1), rdiag1.reshape(HEADS, -1)], axis=1)
    exact = lax.Precision.HIGHEST
    table_enc = jnp.einsum("mb,hm->bh", hot_enc, sums_enc, precision=exact)
    table_dec = jnp.einsum("mb,hm->bh", hot_dec, diag2.reshape(HEADS, -1), precision=exact)
    gains = jnp.stack([gain0, gain1, gain2, gain3, gain4])
    tables = jnp.stack([table_enc, table_dec])
    counts = (across == 0).astype(f32)
    gains, tables = lax.psum((gains * counts, tables * counts), ("dp", "section"))

    def spread_rows(rows, count):
        low = rows.astype(bf16)
        mine = lax.dynamic_slice_in_dim(low, section_id * count, count, 0)
        theirs = lax.dynamic_slice_in_dim(low, (section_id ^ 1) * count, count, 0)
        theirs = swap_section(theirs, 1)
        return jnp.where(core == 0, jnp.stack([mine, theirs]), jnp.stack([theirs, mine]))

    dec_part = DEC // lax.axis_size("section")
    enc_part = BUF // lax.axis_size("section")
    decoder_out = spread_rows(from_owner(out_rows), dec_part)
    decoder_in_grad = spread_rows(from_owner(dec_grad), dec_part)
    encoder_in_grad = spread_rows(from_front(enc_grad.astype(bf16)), enc_part)

    u_enc, u_self, u_cross = (
        u.reshape(4, quarter, D).astype(f32) for u in (unit_enc, unit_self, unit_cross)
    )
    query_grad = jnp.stack([u_enc[0], u_self[0], u_cross[0]])
    keyval_grad = jnp.concatenate([u_enc[1:3], u_self[1:3], u_cross[1:3]])
    output_grad = jnp.stack([u_enc[3], u_self[3], u_cross[3]])
    feed_in_grad = jnp.stack([unit_in1, unit_in2]).astype(f32)
    feed_out_grad = jnp.stack([unit_out1, unit_out2]).astype(f32)
    return (
        decoder_out, encoder_in_grad, decoder_in_grad, query_grad, keyval_grad, output_grad,
        feed_in_grad, feed_out_grad, gains, tables,
    )


def solution(mesh):
    rows = P("dp", None, None)
    mats = P(None, "section", None)
    outs = P("dp", "section", None)
    return jax.shard_map(
        shards,
        mesh=mesh,
        in_specs=(rows, rows, P("dp", None), P("dp", None), mats, mats, mats, mats, mats, P(), P(), rows),
        out_specs=(outs, outs, outs, mats, mats, mats, mats, mats, P(), P()),
        check_vma=False,
    )
```

time: 5790 us -> 548 us (0.09); the launches traced: 5720 us -> 545 us
  local copies, waits for them, and re-layouts: 4190 us -> 61.6 us
  blocking collectives: 501 us -> 41 us
  loops' own time: 189 us -> 0 us
  matrix products: 200 us -> 56.1 us
  waiting for transfers between devices: 362 us -> 243 us
  other arithmetic: 134 us -> 43.4 us
  starting transfers between devices: 131 us -> 53.9 us
    gather x8 -> x0, local copies, waits for them, and re-layouts: 3980 us -> none  [full_bias(): return jnp.take(jnp.transpose(table), bucket, axis=1)]
    psum x2 -> x1, blocking collectives: 501 us -> 41 us  [shards(): lax.psum((gains * counts, tables * counts), ('dp', 'section'))]
    another operation x9 -> x0, loops' own time: 189 us -> none  [the longest x5 156 us: shards(): lax.switch(branch_id, (backward_zero, backward_one, backward_two, backwar...]
    dot_general x48 -> x51, matrix products: 200 us -> 56.1 us  [the longest x16 23.7 us: dot_nt(): lax.dot_general(a, b, (((1,), (1,)), ((), ())), preferred_element_type=f32)]
    all_to_all x2 -> x0, waiting for transfers between devices: 105 us -> none  [the longest x1 105 us: shards(): lax.all_to_all(packed, 'section', split_axis=0, concat_axis=2, tiled=True)]
    ppermute x16 -> x60, starting transfers between devices: 119 us -> 53.9 us  [the longest x35 39.2 us: swap_dp(): return lax.ppermute(value, 'dp', [(i, i ^ bit) for i in range(count)])]
    cond x66 -> x0, local copies, waits for them, and re-layouts: 60.7 us -> none  [the longest x2 49.7 us: shards(): lax.switch(branch_id, (backward_zero, backward_one, backward_two, backwar...]
    ppermute x16 -> x60, waiting for transfers between devices: 256 us -> 243 us  [the longest x35 174 us: swap_dp(): return lax.ppermute(value, 'dp', [(i, i ^ bit) for i in range(count)])]
  transfers between devices with their start and end apart: 21 -> 60, of which waited for: 5 -> 23; matrix products, arithmetic and copies ran while one was open for 21% -> 24% of each run, Pallas kernels for 0% -> 6%
where the time goes in v1:
time: 548 us; the launch traced here: 545 us
  waiting for transfers between devices  243 us (44%)
  local copies, waits for them, and re-layouts  61.6 us (11%)
  matrix products  56.1 us (10%)
  starting transfers between devices  53.9 us (10%)
  other arithmetic  43.4 us (8%)
  blocking collectives  41 us (7%)
  Pallas kernels  37.8 us (7%)
  between operations  7.48 us (1%)
    ppermute x35, waiting for transfers between devices, swap_dp(): return lax.ppermute(value, 'dp', [(i, i ^ bit) for i in range(count)])  174 us
    ppermute x25, waiting for transfers between devices, swap_section(): return lax.ppermute(value, 'section', [(i, i ^ bit) for i in range(count)])  69.4 us
    psum x1, blocking collectives, shards(): lax.psum((gains * counts, tables * counts), ('dp', 'section'))  41 us
    ppermute x35, starting transfers between devices, swap_dp(): return lax.ppermute(value, 'dp', [(i, i ^ bit) for i in range(count)])  39.2 us
    pallas_call x6, Pallas kernels, call(): pl.pallas_call(kernel, grid=(PAIRS,), out_shape=outs, in_specs=in_specs,...  37.8 us
    dot_general x16, matrix products, dot_nt(): lax.dot_general(a, b, (((1,), (1,)), ((), ())), preferred_element_type=f32)  23.7 us
    dynamic_update_slice x9, local copies, waits for them, and re-layouts, gather_mats(): lax.dynamic_update_slice_in_dim(full, piece, (section_id ^ bit) * own.sha...  17.1 us
    dot_general x16, matrix products, dot_nn(): lax.dot_general(a, b, (((1,), (0,)), ((), ())), preferred_element_type=f32)  17.1 us
  transfers between devices with their start and end apart: 60, of which 23 were waited for; matrix products, arithmetic and copies ran while one was open for 24% of the time, Pallas kernels for 6%

profile of v1, /device:TPU:0, one launch (start us, length us, event | category | flops | bytes accessed | tf_op | source)
XLA Modules:
  0.0 544.7 jit_solution(16342192565829901042)
XLA Ops:
  2.3 2.7 fusion.131
  30.4 57.3 %collective-permute-done.7 = bf16[4,192,768]{2,1,0:T(8,128)(2,1)} collective-permute-done((bf16[4,192,768]{2,1,0:T(8,128)(2,1)}, bf16[4,192,768]{2,1,0:T(8,128)(2,1)}, u32[]{:S(2)}, u32[]{:S(2)}) %collective-permute-start.7) | collective-permute-done | bytes 1179680 | tf_op jit(solution)/shard_map/ppermute | solution.py:332
  88.5 3.2 slice_bitcast_fusion.19
  114.6 10.1 %shard_map.232 = (bf16[512,768]{1,0:T(8,128)(2,1)S(1)}, bf16[12,384,384]{2,1,0:T(8,128)(2,1)S(1)}, bf16[12,128,128]{2,1,0:T(8,128)(2,1)S(1)}) custom-call(bf16[512,768]{1,0:T(8,128)(2,1)S(1)} %convolution_convert_fusion.5.q_ref, bf16[512,768]{1,0:T(8,128)(2,1)S(1)} %convolution_convert_fusion.4.k_ref, bf16[512,768]{1,0:T(8,128)(2,1)S(1)} %convolution_convert_fusion.3.v_ref, ...), custom_call_target="tpu_custom_call" | custom-call | flops 4000000000 | bytes 8388608 | tf_op jit(solution)/shard_map/pallas_call | solution.py:184
  138.0 4.3 shard_map.231
  143.9 9.8 %collective-permute-done.11 = bf16[512,768]{1,0:T(8,128)(2,1)S(1)} collective-permute-done((bf16[512,768]{1,0:T(8,128)(2,1)S(1)}, bf16[512,768]{1,0:T(8,128)(2,1)S(1)}, u32[]{:S(2)}, u32[]{:S(2)}) %collective-permute-start.11) | collective-permute-done | bytes 786464 | tf_op jit(solution)/shard_map/ppermute | solution.py:332
  155.7 5.7 %shard_map.233 = (bf16[96,768]{1,0:T(8,128)(2,1)S(1)}, bf16[12,512,96]{2,1,0:T(8,128)(2,1)S(1)}) custom-call(bf16[96,768]{1,0:T(8,128)(2,1)S(1)} %convolution_convert_fusion.20.refs_0_, bf16[512,768]{1,0:T(8,128)(2,1)S(1)} %convolution_convert_fusion.2.refs_1_, bf16[512,768]{1,0:T(8,128)(2,1)S(1)} %convolution_convert_fusion.1.refs_2_), custom_call_target="tpu_custom_call" | custom-call | flops 2000000000 | bytes 8388608 | tf_op jit(solution)/shard_map/pallas_call | solution.py:184
  176.2 4.8 shard_map.234
  188.2 3.1 shard_map.236
  195.6 4.4 fusion.6
  230.6 9.8 %shard_map.235 = (bf16[512,768]{1,0:T(8,128)(2,1)S(1)}, bf16[512,768]{1,0:T(8,128)(2,1)S(1)}, bf16[512,768]{1,0:T(8,128)(2,1)S(1)}, f32[12,3,512]{2,1,0:T(4,128)S(1)}, f32[12,1,256]{2,1,0:T(1,128)S(1)}) custom-call(bf16[512,768]{1,0:T(8,128)(2,1)S(1)} %convolution_convert_fusion.5.q_ref, bf16[512,768]{1,0:T(8,128)(2,1)S(1)} %convolution_convert_fusion.4.k_ref, ...), custom_call_target="tpu_custom_call" | custom-call | flops 8999999488 | bytes 8388608 | tf_op jit(solution)/shard_map/pallas_call | solution.py:184
  256.9 41.0 %all-reduce = (f32[5,768]{1,0:T(8,128)}, f32[2,32,12]{1,2,0:T(8,128)S(1)}) all-reduce(f32[5,768]{1,0:T(8,128)S(1)} %broadcast_multiply_fusion, f32[2,32,12]{1,2,0:T(8,128)S(1)} %maximum_multiply_fusion), channel_id=1, replica_groups=mesh['dp'=8,'section'=4] {'dp','section'}, use_global_device_ids=true, to_apply=%region_18.19 | all-reduce | flops 4608 | bytes 36864 | tf_op jit(solution)/shard_map/psum | solution.py:522
  305.4 2.6 collective-permute-start.43
  316.1 6.2 %collective-permute-done.43 = bf16[384,768]{1,0:T(8,128)(2,1)S(1)} collective-permute-done((bf16[384,768]{1,0:T(8,128)(2,1)S(1)}, bf16[384,768]{1,0:T(8,128)(2,1)S(1)}, u32[]{:S(2)}, u32[]{:S(2)}) %collective-permute-start.43) | collective-permute-done | bytes 589856 | tf_op jit(solution)/shard_map/ppermute | solution.py:337
  327.0 7.9 %collective-permute-done.31 = bf16[384,768]{1,0:T(8,128)(2,1)S(1)} collective-permute-done((bf16[384,768]{1,0:T(8,128)(2,1)S(1)}, bf16[384,768]{1,0:T(8,128)(2,1)S(1)}, u32[]{:S(2)}, u32[]{:S(2)}) %collective-permute-start.31) | collective-permute-done | bytes 589856 | tf_op jit(solution)/shard_map/ppermute | solution.py:337
  336.6 10.9 %collective-permute-done.25 = bf16[384,768]{1,0:T(8,128)(2,1)S(1)} collective-permute-done((bf16[384,768]{1,0:T(8,128)(2,1)S(1)}, bf16[384,768]{1,0:T(8,128)(2,1)S(1)}, u32[]{:S(2)}, u32[]{:S(2)}) %collective-permute-start.25) | collective-permute-done | bytes 589856 | tf_op jit(solution)/shard_map/ppermute | solution.py:337
  350.0 9.8 %collective-permute-done.37 = bf16[384,768]{1,0:T(8,128)(2,1)S(1)} collective-permute-done((bf16[384,768]{1,0:T(8,128)(2,1)S(1)}, bf16[384,768]{1,0:T(8,128)(2,1)S(1)}, u32[]{:S(2)}, u32[]{:S(2)}) %collective-permute-start.37) | collective-permute-done | bytes 589856 | tf_op jit(solution)/shard_map/ppermute | solution.py:337
  367.5 14.8 %collective-permute-done.32 = bf16[192,768]{1,0:T(8,128)(2,1)S(1)} collective-permute-done((bf16[192,768]{1,0:T(8,128)(2,1)S(1)}, bf16[192,768]{1,0:T(8,128)(2,1)S(1)}, u32[]{:S(2)}, u32[]{:S(2)}) %collective-permute-start.32) | collective-permute-done | bytes 294944 | tf_op jit(solution)/shard_map/ppermute | solution.py:337
  384.2 4.4 collective-permute-done.26
  390.5 4.1 collective-permute-done.38
  395.1 2.7 collective-permute-start.27
  400.0 23.0 %collective-permute-done.33 = bf16[192,768]{1,0:T(8,128)(2,1)S(1)} collective-permute-done((bf16[192,768]{1,0:T(8,128)(2,1)S(1)}, bf16[192,768]{1,0:T(8,128)(2,1)S(1)}, u32[]{:S(2)}, u32[]{:S(2)}) %collective-permute-start.33) | collective-permute-done | bytes 294944 | tf_op jit(solution)/shard_map/ppermute | solution.py:337
  423.0 6.3 %collective-permute-done.27 = bf16[192,768]{1,0:T(8,128)(2,1)S(1)} collective-permute-done((bf16[192,768]{1,0:T(8,128)(2,1)S(1)}, bf16[192,768]{1,0:T(8,128)(2,1)S(1)}, u32[]{:S(2)}, u32[]{:S(2)}) %collective-permute-start.27) | collective-permute-done | bytes 294944 | tf_op jit(solution)/shard_map/ppermute | solution.py:337
  429.4 12.5 %collective-permute-done.39 = bf16[192,768]{1,0:T(8,128)(2,1)S(1)} collective-permute-done((bf16[192,768]{1,0:T(8,128)(2,1)S(1)}, bf16[192,768]{1,0:T(8,128)(2,1)S(1)}, u32[]{:S(2)}, u32[]{:S(2)}) %collective-permute-start.39) | collective-permute-done | bytes 294944 | tf_op jit(solution)/shard_map/ppermute | solution.py:337
  444.5 3.8 collective-permute-done.58
  450.0 10.9 %collective-permute-done.34 = bf16[192,768]{1,0:T(8,128)(2,1)S(1)} collective-permute-done((bf16[192,768]{1,0:T(8,128)(2,1)S(1)}, bf16[192,768]{1,0:T(8,128)(2,1)S(1)}, u32[]{:S(2)}, u32[]{:S(2)}) %collective-permute-start.34) | collective-permute-done | bytes 294944 | tf_op jit(solution)/shard_map/ppermute | solution.py:337
  461.1 6.1 %collective-permute-done.28 = bf16[192,768]{1,0:T(8,128)(2,1)S(1)} collective-permute-done((bf16[192,768]{1,0:T(8,128)(2,1)S(1)}, bf16[192,768]{1,0:T(8,128)(2,1)S(1)}, u32[]{:S(2)}, u32[]{:S(2)}) %collective-permute-start.28) | collective-permute-done | bytes 294944 | tf_op jit(solution)/shard_map/ppermute | solution.py:337
  467.4 6.1 %collective-permute-done.40 = bf16[192,768]{1,0:T(8,128)(2,1)S(1)} collective-permute-done((bf16[192,768]{1,0:T(8,128)(2,1)S(1)}, bf16[192,768]{1,0:T(8,128)(2,1)S(1)}, u32[]{:S(2)}, u32[]{:S(2)}) %collective-permute-start.40) | collective-permute-done | bytes 294944 | tf_op jit(solution)/shard_map/ppermute | solution.py:337
  474.9 4.9 collective-permute-done.20
  481.4 17.3 %collective-permute-done.59 = bf16[384,768]{1,0:T(8,128)(2,1)S(1)} collective-permute-done((bf16[384,768]{1,0:T(8,128)(2,1)S(1)}, bf16[384,768]{1,0:T(8,128)(2,1)S(1)}, u32[]{:S(2)}, u32[]{:S(2)}) %collective-permute-start.59) | collective-permute-done | bytes 589856 | tf_op jit(solution)/shard_map/ppermute | solution.py:337
  506.4 10.4 %collective-permute-done.53 = bf16[384,768]{1,0:T(8,128)(2,1)S(1)} collective-permute-done((bf16[384,768]{1,0:T(8,128)(2,1)S(1)}, bf16[384,768]{1,0:T(8,128)(2,1)S(1)}, u32[]{:S(2)}, u32[]{:S(2)}) %collective-permute-start.53) | collective-permute-done | bytes 589856 | tf_op jit(solution)/shard_map/ppermute | solution.py:337
  524.5 11.6 %collective-permute-done.23 = bf16[384,768]{1,0:T(8,128)(2,1)S(1)} collective-permute-done((bf16[384,768]{1,0:T(8,128)(2,1)S(1)}, bf16[384,768]{1,0:T(8,128)(2,1)S(1)}, u32[]{:S(2)}, u32[]{:S(2)}) %collective-permute-start.23) | collective-permute-done | bytes 589856 | tf_op jit(solution)/shard_map/ppermute | solution.py:337
  (497 shorter events, 204.8 us)
Async XLA Ops:
  7.7 89.6 %collective-permute-start.1 = (bf16[4,192,768]{2,1,0:T(8,128)(2,1)}, bf16[4,192,768]{2,1,0:T(8,128)(2,1)}, u32[]{:S(2)}, u32[]{:S(2)}) collective-permute-start(bf16[4,192,768]{2,1,0:T(8,128)(2,1)} %get-tuple-element.120), channel_id=1, source_target_pairs={{0,2},{1,3},{2,0},{3,1},{4,6},{5,7},{6,4},{7,5},{8,10},{9,11},{10,... | collective-permute-start | bytes 3538952 | tf_op jit(solution)/shard_map/ppermute | solution.py:332
  12.4 81.8 %collective-permute-start.3 = (bf16[4,192,768]{2,1,0:T(8,128)(2,1)}, bf16[4,192,768]{2,1,0:T(8,128)(2,1)}, u32[]{:S(2)}, u32[]{:S(2)}) collective-permute-start(bf16[4,192,768]{2,1,0:T(8,128)(2,1)} %get-tuple-element.118), channel_id=1, source_target_pairs={{0,1},{1,0},{2,3},{3,2},{4,5},{5,4},{6,7},{7,6},{8,9},{9,8},{10,11... | collective-permute-start | bytes 3538952 | tf_op jit(solution)/shard_map/ppermute | solution.py:332
  12.6 87.1 %collective-permute-start.4 = (bf16[4,192,768]{2,1,0:T(8,128)(2,1)}, bf16[4,192,768]{2,1,0:T(8,128)(2,1)}, u32[]{:S(2)}, u32[]{:S(2)}) collective-permute-start(bf16[4,192,768]{2,1,0:T(8,128)(2,1)} %get-tuple-element.118), channel_id=1, source_target_pairs={{0,2},{1,3},{2,0},{3,1},{4,6},{5,7},{6,4},{7,5},{8,10},{9,11},{10,... | collective-permute-start | bytes 3538952 | tf_op jit(solution)/shard_map/ppermute | solution.py:332
  17.6 70.1 %collective-permute-start.7 = (bf16[4,192,768]{2,1,0:T(8,128)(2,1)}, bf16[4,192,768]{2,1,0:T(8,128)(2,1)}, u32[]{:S(2)}, u32[]{:S(2)}) collective-permute-start(bf16[4,192,768]{2,1,0:T(8,128)(2,1)} %get-tuple-element.116), channel_id=1, source_target_pairs={{0,2},{1,3},{2,0},{3,1},{4,6},{5,7},{6,4},{7,5},{8,10},{9,11},{10,... | collective-permute-start | bytes 3538952 | tf_op jit(solution)/shard_map/ppermute | solution.py:332
  29.7 72.8 %collective-permute-start.6 = (bf16[4,192,768]{2,1,0:T(8,128)(2,1)}, bf16[4,192,768]{2,1,0:T(8,128)(2,1)S(1)}, u32[]{:S(2)}, u32[]{:S(2)}) collective-permute-start(bf16[4,192,768]{2,1,0:T(8,128)(2,1)} %get-tuple-element.116), channel_id=1, source_target_pairs={{0,1},{1,0},{2,3},{3,2},{4,5},{5,4},{6,7},{7,6},{8,9},{9,8},{10,11... | collective-permute-start | bytes 3538952 | tf_op jit(solution)/shard_map/ppermute | solution.py:332
  94.2 32.7 %collective-permute-start.10 = (bf16[2,768,768]{2,1,0:T(8,128)(2,1)S(1)}, bf16[2,768,768]{2,1,0:T(8,128)(2,1)S(1)}, u32[]{:S(2)}, u32[]{:S(2)}) collective-permute-start(bf16[2,768,768]{2,1,0:T(8,128)(2,1)S(1)} %copy-done.14), channel_id=1, source_target_pairs={{0,1},{1,0},{2,3},{3,2},{4,5},{5,4},{6,7},{7,6},{8,9},{9,8},{10,11... | collective-permute-start | bytes 7077896 | tf_op jit(solution)/shard_map/ppermute | solution.py:332
  97.3 30.8 %collective-permute-start.9 = (bf16[2,768,768]{2,1,0:T(8,128)(2,1)S(1)}, bf16[2,768,768]{2,1,0:T(8,128)(2,1)S(1)}, u32[]{:S(2)}, u32[]{:S(2)}) collective-permute-start(bf16[2,768,768]{2,1,0:T(8,128)(2,1)S(1)} %copy-done.15), channel_id=1, source_target_pairs={{0,1},{1,0},{2,3},{3,2},{4,5},{5,4},{6,7},{7,6},{8,9},{9,8},{10,11... | collective-permute-start | bytes 7077896 | tf_op jit(solution)/shard_map/ppermute | solution.py:332
  99.7 35.9 %collective-permute-start.2 = (bf16[4,192,768]{2,1,0:T(8,128)(2,1)}, bf16[4,192,768]{2,1,0:T(8,128)(2,1)}, u32[]{:S(2)}, u32[]{:S(2)}) collective-permute-start(bf16[4,192,768]{2,1,0:T(8,128)(2,1)} %collective-permute-done.1), channel_id=1, source_target_pairs={{0,1},{1,0},{2,3},{3,2},{4,5},{5,4},{6,7},{7,6},{8,9},{9,8},{10,11... | collective-permute-start | bytes 3538952 | tf_op jit(solution)/shard_map/ppermute | solution.py:332
  102.5 40.3 %collective-permute-start.5 = (bf16[4,192,768]{2,1,0:T(8,128)(2,1)}, bf16[4,192,768]{2,1,0:T(8,128)(2,1)S(1)}, u32[]{:S(2)}, u32[]{:S(2)}) collective-permute-start(bf16[4,192,768]{2,1,0:T(8,128)(2,1)} %collective-permute-done.4), channel_id=1, source_target_pairs={{0,1},{1,0},{2,3},{3,2},{4,5},{5,4},{6,7},{7,6},{8,9},{9,8},{10,11... | collective-permute-start | bytes 3538952 | tf_op jit(solution)/shard_map/ppermute | solution.py:332
  171.6 31.0 %collective-permute-start.12 = (bf16[96,768]{1,0:T(8,128)(2,1)}, bf16[96,768]{1,0:T(8,128)(2,1)}, u32[]{:S(2)}, u32[]{:S(2)}) collective-permute-start(bf16[96,768]{1,0:T(8,128)(2,1)} %fusion.53), channel_id=1, source_target_pairs={{0,2},{1,3},{2,0},{3,1},{4,6},{5,7},{6,4},{7,5},{8,10},{9,11},{10,... | collective-permute-start | bytes 442376 | tf_op jit(solution)/shard_map/ppermute | solution.py:332
  173.7 127.0 %collective-permute-start.42 = (bf16[768,768]{1,0:T(8,128)(2,1)}, bf16[768,768]{1,0:T(8,128)(2,1)}, u32[]{:S(2)}, u32[]{:S(2)}) collective-permute-start(bf16[768,768]{1,0:T(8,128)(2,1)} %slice.436), channel_id=1, source_target_pairs={{0,1},{1,0},{2,3},{3,2},{4,5},{5,4},{6,7},{7,6},{8,9},{9,8},{10,11... | collective-permute-start | bytes 3538952 | tf_op jit(solution)/shard_map/ppermute | solution.py:332
  174.8 128.5 %collective-permute-start.54 = (bf16[768,768]{1,0:T(8,128)(2,1)}, bf16[768,768]{1,0:T(8,128)(2,1)}, u32[]{:S(2)}, u32[]{:S(2)}) collective-permute-start(bf16[768,768]{1,0:T(8,128)(2,1)} %slice.434), channel_id=1, source_target_pairs={{0,1},{1,0},{2,3},{3,2},{4,5},{5,4},{6,7},{7,6},{8,9},{9,8},{10,11... | collective-permute-start | bytes 3538952 | tf_op jit(solution)/shard_map/ppermute | solution.py:332
  222.7 82.8 %collective-permute-start.30 = (bf16[768,768]{1,0:T(8,128)(2,1)}, bf16[768,768]{1,0:T(8,128)(2,1)}, u32[]{:S(2)}, u32[]{:S(2)}) collective-permute-start(bf16[768,768]{1,0:T(8,128)(2,1)} %pad_maximum_fusion.24), channel_id=1, source_target_pairs={{0,1},{1,0},{2,3},{3,2},{4,5},{5,4},{6,7},{7,6},{8,9},{9,8},{10,11... | collective-permute-start | bytes 3538952 | tf_op jit(solution)/shard_map/ppermute | solution.py:332
  223.7 86.2 %collective-permute-start.24 = (bf16[768,768]{1,0:T(8,128)(2,1)}, bf16[768,768]{1,0:T(8,128)(2,1)}, u32[]{:S(2)}, u32[]{:S(2)}) collective-permute-start(bf16[768,768]{1,0:T(8,128)(2,1)} %pad_maximum_fusion.23), channel_id=1, source_target_pairs={{0,1},{1,0},{2,3},{3,2},{4,5},{5,4},{6,7},{7,6},{8,9},{9,8},{10,11... | collective-permute-start | bytes 3538952 | tf_op jit(solution)/shard_map/ppermute | solution.py:332
  250.9 47.8 %collective-permute-start.16 = (bf16[128,768]{1,0:T(8,128)(2,1)}, bf16[128,768]{1,0:T(8,128)(2,1)}, u32[]{:S(2)}, u32[]{:S(2)}) collective-permute-start(bf16[128,768]{1,0:T(8,128)(2,1)} %get-tuple-element.129), channel_id=1, source_target_pairs={{0,1},{1,0},{2,3},{3,2},{4,5},{5,4},{6,7},{7,6},{8,9},{9,8},{10,11... | collective-permute-start | bytes 589832 | tf_op jit(solution)/shard_map/ppermute | solution.py:332
  303.3 62.2 %collective-permute-start.18 = (bf16[768,768]{1,0:T(8,128)(2,1)S(1)}, bf16[768,768]{1,0:T(8,128)(2,1)S(1)}, u32[]{:S(2)}, u32[]{:S(2)}) collective-permute-start(bf16[768,768]{1,0:T(8,128)(2,1)S(1)} %pad_maximum_fusion.22), channel_id=1, source_target_pairs={{0,1},{1,0},{2,3},{3,2},{4,5},{5,4},{6,7},{7,6},{8,9},{9,8},{10,11... | collective-permute-start | bytes 3538952 | tf_op jit(solution)/shard_map/ppermute | solution.py:332
  314.5 33.0 %collective-permute-start.25 = (bf16[384,768]{1,0:T(8,128)(2,1)S(1)}, bf16[384,768]{1,0:T(8,128)(2,1)S(1)}, u32[]{:S(2)}, u32[]{:S(2)}) collective-permute-start(bf16[384,768]{1,0:T(8,128)(2,1)S(1)} %constant_dynamic-slice_fusion.19), channel_id=1, source_target_pairs={{0,4},{4,0},{8,12},{12,8},{16,20},{20,16},{24,28},{28,24},{1,5},{5... | collective-permute-start | bytes 1769480 | tf_op jit(solution)/shard_map/ppermute | solution.py:337
  322.2 37.6 %collective-permute-start.37 = (bf16[384,768]{1,0:T(8,128)(2,1)S(1)}, bf16[384,768]{1,0:T(8,128)(2,1)S(1)}, u32[]{:S(2)}, u32[]{:S(2)}) collective-permute-start(bf16[384,768]{1,0:T(8,128)(2,1)S(1)} %constant_dynamic-slice_fusion.7), channel_id=1, source_target_pairs={{0,4},{4,0},{8,12},{12,8},{16,20},{20,16},{24,28},{28,24},{1,5},{5... | collective-permute-start | bytes 1769480 | tf_op jit(solution)/shard_map/ppermute | solution.py:337
  325.3 36.2 %collective-permute-start.49 = (bf16[384,768]{1,0:T(8,128)(2,1)S(1)}, bf16[384,768]{1,0:T(8,128)(2,1)S(1)}, u32[]{:S(2)}, u32[]{:S(2)}) collective-permute-start(bf16[384,768]{1,0:T(8,128)(2,1)S(1)} %constant_dynamic-slice_fusion.3), channel_id=1, source_target_pairs={{0,8},{4,12},{8,0},{12,4},{16,24},{20,28},{24,16},{28,20},{1,9},{5... | collective-permute-start | bytes 1769480 | tf_op jit(solution)/shard_map/ppermute | solution.py:337
  362.4 32.3 %collective-permute-start.38 = (bf16[192,768]{1,0:T(8,128)(2,1)S(1)}, bf16[192,768]{1,0:T(8,128)(2,1)S(1)}, u32[]{:S(2)}, u32[]{:S(2)}) collective-permute-start(bf16[192,768]{1,0:T(8,128)(2,1)S(1)} %constant_dynamic-slice_fusion.6), channel_id=1, source_target_pairs={{0,8},{4,12},{8,0},{12,4},{16,24},{20,28},{24,16},{28,20},{1,9},{5... | collective-permute-start | bytes 884744 | tf_op jit(solution)/shard_map/ppermute | solution.py:337
  364.0 31.0 %collective-permute-start.50 = (bf16[192,768]{1,0:T(8,128)(2,1)S(1)}, bf16[192,768]{1,0:T(8,128)(2,1)S(1)}, u32[]{:S(2)}, u32[]{:S(2)}) collective-permute-start(bf16[192,768]{1,0:T(8,128)(2,1)S(1)} %constant_dynamic-slice_fusion.2), channel_id=1, source_target_pairs={{0,16},{4,20},{8,24},{12,28},{16,0},{20,4},{24,8},{28,12},{1,17},{... | collective-permute-start | bytes 884744 | tf_op jit(solution)/shard_map/ppermute | solution.py:337
  365.5 32.4 %collective-permute-start.45 = (bf16[192,768]{1,0:T(8,128)(2,1)S(1)}, bf16[192,768]{1,0:T(8,128)(2,1)S(1)}, u32[]{:S(2)}, u32[]{:S(2)}) collective-permute-start(bf16[192,768]{1,0:T(8,128)(2,1)S(1)} %add_convert_fusion.16), channel_id=1, source_target_pairs={{0,16},{4,20},{8,24},{12,28},{16,0},{20,4},{24,8},{28,12},{1,17},{... | collective-permute-start | bytes 884744 | tf_op jit(solution)/shard_map/ppermute | solution.py:337
  388.6 59.8 %collective-permute-start.19 = (bf16[384,768]{1,0:T(8,128)(2,1)S(1)}, bf16[384,768]{1,0:T(8,128)(2,1)S(1)}, u32[]{:S(2)}, u32[]{:S(2)}) collective-permute-start(bf16[384,768]{1,0:T(8,128)(2,1)S(1)} %constant_dynamic-slice_fusion.29), channel_id=1, source_target_pairs={{0,4},{4,0},{8,12},{12,8},{16,20},{20,16},{24,28},{28,24},{1,5},{5... | collective-permute-start | bytes 1769480 | tf_op jit(solution)/shard_map/ppermute | solution.py:337
  394.7 28.3 %collective-permute-start.33 = (bf16[192,768]{1,0:T(8,128)(2,1)S(1)}, bf16[192,768]{1,0:T(8,128)(2,1)S(1)}, u32[]{:S(2)}, u32[]{:S(2)}) collective-permute-start(bf16[192,768]{1,0:T(8,128)(2,1)S(1)} %add_convert_fusion.20), channel_id=1, source_target_pairs={{0,16},{4,20},{8,24},{12,28},{16,0},{20,4},{24,8},{28,12},{1,17},{... | collective-permute-start | bytes 884744 | tf_op jit(solution)/shard_map/ppermute | solution.py:337
  395.1 34.3 %collective-permute-start.27 = (bf16[192,768]{1,0:T(8,128)(2,1)S(1)}, bf16[192,768]{1,0:T(8,128)(2,1)S(1)}, u32[]{:S(2)}, u32[]{:S(2)}) collective-permute-start(bf16[192,768]{1,0:T(8,128)(2,1)S(1)} %add_convert_fusion.22), channel_id=1, source_target_pairs={{0,16},{4,20},{8,24},{12,28},{16,0},{20,4},{24,8},{28,12},{1,17},{... | collective-permute-start | bytes 884744 | tf_op jit(solution)/shard_map/ppermute | solution.py:337
  397.9 44.1 %collective-permute-start.39 = (bf16[192,768]{1,0:T(8,128)(2,1)S(1)}, bf16[192,768]{1,0:T(8,128)(2,1)S(1)}, u32[]{:S(2)}, u32[]{:S(2)}) collective-permute-start(bf16[192,768]{1,0:T(8,128)(2,1)S(1)} %add_convert_fusion.18), channel_id=1, source_target_pairs={{0,16},{4,20},{8,24},{12,28},{16,0},{20,4},{24,8},{28,12},{1,17},{... | collective-permute-start | bytes 884744 | tf_op jit(solution)/shard_map/ppermute | solution.py:337
  398.3 43.7 %collective-permute-start.51 = (bf16[192,768]{1,0:T(8,128)(2,1)S(1)}, bf16[192,768]{1,0:T(8,128)(2,1)S(1)}, u32[]{:S(2)}, u32[]{:S(2)}) collective-permute-start(bf16[192,768]{1,0:T(8,128)(2,1)S(1)} %add_convert_fusion.14), channel_id=1, source_target_pairs={{0,4},{4,0},{8,12},{12,8},{16,20},{20,16},{24,28},{28,24},{1,5},{5... | collective-permute-start | bytes 884744 | tf_op jit(solution)/shard_map/ppermute | solution.py:337
  444.2 29.3 %collective-permute-start.40 = (bf16[192,768]{1,0:T(8,128)(2,1)S(1)}, bf16[192,768]{1,0:T(8,128)(2,1)S(1)}, u32[]{:S(2)}, u32[]{:S(2)}) collective-permute-start(bf16[192,768]{1,0:T(8,128)(2,1)S(1)} %add_convert_fusion.17), channel_id=1, source_target_pairs={{0,8},{4,12},{8,0},{12,4},{16,24},{20,28},{24,16},{28,20},{1,9},{5... | collective-permute-start | bytes 884744 | tf_op jit(solution)/shard_map/ppermute | solution.py:337
  448.3 32.9 %collective-permute-start.52 = (bf16[192,768]{1,0:T(8,128)(2,1)S(1)}, bf16[192,768]{1,0:T(8,128)(2,1)S(1)}, u32[]{:S(2)}, u32[]{:S(2)}) collective-permute-start(bf16[192,768]{1,0:T(8,128)(2,1)S(1)} %add_convert_fusion.13), channel_id=1, source_target_pairs={{0,16},{4,20},{8,24},{12,28},{16,0},{20,4},{24,8},{28,12},{1,17},{... | collective-permute-start | bytes 884744 | tf_op jit(solution)/shard_map/ppermute | solution.py:337
  448.5 51.9 %collective-permute-start.47 = (bf16[384,768]{1,0:T(8,128)(2,1)S(1)}, bf16[384,768]{1,0:T(8,128)(2,1)S(1)}, u32[]{:S(2)}, u32[]{:S(2)}) collective-permute-start(bf16[384,768]{1,0:T(8,128)(2,1)S(1)} %maximum_select_fusion.11), channel_id=1, source_target_pairs={{0,4},{4,0},{8,12},{12,8},{16,20},{20,16},{24,28},{28,24},{1,5},{5... | collective-permute-start | bytes 1769480 | tf_op jit(solution)/shard_map/ppermute | solution.py:337
  467.2 31.5 %collective-permute-start.59 = (bf16[384,768]{1,0:T(8,128)(2,1)S(1)}, bf16[384,768]{1,0:T(8,128)(2,1)S(1)}, u32[]{:S(2)}, u32[]{:S(2)}) collective-permute-start(bf16[384,768]{1,0:T(8,128)(2,1)S(1)} %maximum_select_fusion.13), channel_id=1, source_target_pairs={{0,8},{4,12},{8,0},{12,4},{16,24},{20,28},{24,16},{28,20},{1,9},{5... | collective-permute-start | bytes 1769480 | tf_op jit(solution)/shard_map/ppermute | solution.py:337
  473.5 32.6 %collective-permute-start.35 = (bf16[384,768]{1,0:T(8,128)(2,1)S(1)}, bf16[384,768]{1,0:T(8,128)(2,1)S(1)}, u32[]{:S(2)}, u32[]{:S(2)}) collective-permute-start(bf16[384,768]{1,0:T(8,128)(2,1)S(1)} %maximum_select_fusion.9), channel_id=1, source_target_pairs={{0,4},{4,0},{8,12},{12,8},{16,20},{20,16},{24,28},{28,24},{1,5},{5... | collective-permute-start | bytes 1769480 | tf_op jit(solution)/shard_map/ppermute | solution.py:337
  (117 other events, 1079.2 us)
